TPU v7x, 512 devices: a whole 4x8x8 slice. The times are simulated.
512 devices in a mesh: blk: 128 (over x, z_hi, y, core), grp: 4 (over z_lo).
Axes of the slice: x: 4, y: 8, z: 8 (z_hi: 2, z_lo: 4; z = z_hi * 4 + z_lo), core: 2. Of those that a mesh axis runs over, the one named last changes fastest.
Arguments:
- source_emb: float32 [128, 512, 400], P('blk', 'grp'), may hold values from -1.2 to 1.2
- source_state: float32 [128, 512], P('blk', 'grp'), may hold values from 0.01 to 0.1
- target_emb: float32 [128, 512, 400], P('blk', 'grp'), may hold values from -1.2 to 1.2
- target_state: float32 [128, 512], P('blk', 'grp'), may hold values from 0.01 to 0.1
- relation_emb: float32 [512, 400], replicated, may hold values from 0.1 to 1.9
- relation_state: float32 [512], replicated, may hold values from 0.01 to 0.1
- source_ids: int32 [2, 128, 4, 512], P(None, 'blk', 'grp'), may hold values from 0 to 127
- target_ids: int32 [2, 128, 4, 512], P(None, 'blk', 'grp'), may hold values from 0 to 127
- relation_ids: int32 [2, 128, 4, 512], P(None, 'blk', 'grp'), may hold values from 0 to 511
- edge_counts: int32 [2, 128, 4], P(None, 'blk', 'grp'), may hold values from 128 to 512, as said below
- sample_ids: int32 [2, 128, 4, 1, 256], P(None, 'blk', 'grp'), may hold values from 0 to 127
Outputs:
- source_out: float32 [128, 512, 400], P('blk', 'grp')
- source_state_out: float32 [128, 512], P('blk', 'grp')
- target_out: float32 [128, 512, 400], P('blk', 'grp')
- target_state_out: float32 [128, 512], P('blk', 'grp')
- relation_out: float32 [512, 400], replicated
- relation_state_out: float32 [512], replicated
Inputs may be any that keep to these rules, and one draw needn't show every extreme that they name: `edge_counts`: in every round some bucket is full.
All inputs are finite; a program needn't handle non-finite values.
Results may differ from a plain program's by a relative error of at most 0.0003.
Values sent between devices are 32-bit elements; how exact they have to be, the bound alone decides.
No kernel may reach another device: no remote copies, remote signals or barrier semaphores. Data moves between devices by JAX's collectives and lax.ppermute only.
A program may use at most 64 MiB of HBM per device.

v0:
```python
import jax
import jax.numpy as jnp
from jax import lax
from jax.sharding import PartitionSpec as P

learning_rate = 0.1
relation_rate = 0.1


def passed_along(block, axis, distance):
    devices = range(lax.axis_size(axis))
    route = [((i - distance) % len(devices), i) for i in devices]
    return lax.ppermute(block, axis, route)


def adagrad(weights, accum, grads, rate):
    fresh = accum + jnp.mean(grads * grads, axis=-1)
    return (weights - rate * grads * lax.rsqrt(fresh)[..., None], fresh)


def pick_rows(selector, table):
    return jnp.dot(selector, table, precision=lax.Precision.HIGHEST)


def put_rows(selector, values):
    return jnp.einsum("ir,id->rd", selector, values, precision=lax.Precision.HIGHEST)


def on_device(
    source_emb,
    source_state,
    target_emb,
    target_state,
    relation_emb,
    relation_state,
    source_ids,
    target_ids,
    relation_ids,
    edge_counts,
    sample_ids,
):
    source_rows = source_emb[0]
    source_acc = source_state[0]
    target_rows = target_emb[0]
    target_acc = target_state[0]
    rounds = source_ids.shape[0]
    slots = source_ids.shape[3]
    blocks = sample_ids.shape[3]
    samples = sample_ids.shape[4]
    per_block = slots // blocks
    slab_rows = source_rows.shape[0]
    kinds = relation_emb.shape[0]
    row_iota = jnp.arange(slab_rows, dtype=jnp.int32)
    total = jnp.zeros(relation_emb.shape, jnp.float32)
    for round_index in range(rounds):
        these_source = source_ids[round_index, 0, 0]
        these_target = target_ids[round_index, 0, 0]
        these_kinds = relation_ids[round_index, 0, 0]
        these_samples = sample_ids[round_index, 0, 0]
        live_count = edge_counts[round_index, 0, 0]
        held_source = source_rows
        held_target = target_rows

        def visit(block_index, running):
            grad_source, grad_target, grad_relation = running
            first = block_index * per_block
            picked_samples = lax.dynamic_index_in_dim(these_samples, block_index, 0, keepdims=False)
            alive = (first + jnp.arange(per_block, dtype=jnp.int32) < live_count).astype(
                jnp.float32
            )
            source_hot = (these_source[:, None] == row_iota[None, :]).astype(jnp.float32)
            target_hot = (these_target[:, None] == row_iota[None, :]).astype(jnp.float32)
            sample_hot = (picked_samples[:, None] == row_iota[None, :]).astype(jnp.float32)
            scale = relation_emb[these_kinds]
            left = pick_rows(source_hot, held_source)
            right = pick_rows(target_hot, held_target)
            sampled = pick_rows(sample_hot, held_target)
            query = left * scale
            positive = jnp.sum(query * right, axis=-1)
            negative = jnp.einsum("id,jd->ij", query, sampled, precision=lax.Precision.HIGHEST)
            pull = -alive * jax.nn.sigmoid(-positive)
            push = alive[:, None] * jax.nn.sigmoid(negative) / samples
            grad_query = pull[:, None] * right + jnp.dot(
                push, sampled, precision=lax.Precision.HIGHEST
            )
            grad_source = grad_source + put_rows(source_hot, grad_query * scale)
            to_samples = jnp.einsum("ij,id->jd", push, query, precision=lax.Precision.HIGHEST)
            grad_target = (
                grad_target
                + put_rows(target_hot, pull[:, None] * query)
                + put_rows(sample_hot, to_samples)
            )
            grad_relation = grad_relation + jax.ops.segment_sum(
                grad_query * left, these_kinds, num_segments=kinds
            )
            return (grad_source, grad_target, grad_relation)

        initial = (
            jnp.zeros_like(source_rows),
            jnp.zeros_like(target_rows),
            jnp.zeros(relation_emb.shape, jnp.float32),
        )
        grad_source, grad_target, grad_relation = lax.fori_loop(0, blocks, visit, initial)
        total = total + lax.psum(grad_relation, ("blk", "grp"))
        target_rows, target_acc = adagrad(target_rows, target_acc, grad_target, learning_rate)
        source_rows, source_acc = adagrad(source_rows, source_acc, grad_source, learning_rate)
        if round_index + 1 < rounds:
            source_rows, source_acc = passed_along((source_rows, source_acc), "blk", 1)
    relation_out, relation_state_out = adagrad(relation_emb, relation_state, total, relation_rate)
    return (
        source_rows[None],
        source_acc[None],
        target_rows[None],
        target_acc[None],
        relation_out,
        relation_state_out,
    )


def solution(mesh):
    in_specs = (
        P("blk", "grp", None),
        P("blk", "grp"),
        P("blk", "grp", None),
        P("blk", "grp"),
        P(),
        P(),
        P(None, "blk", "grp", None),
        P(None, "blk", "grp", None),
        P(None, "blk", "grp", None),
        P(None, "blk", "grp"),
        P(None, "blk", "grp", None, None),
    )
    out_specs = (
        P("blk", "grp", None),
        P("blk", "grp"),
        P("blk", "grp", None),
        P("blk", "grp"),
        P(),
        P(),
    )
    return jax.shard_map(
        on_device, mesh=mesh, in_specs=in_specs, out_specs=out_specs, check_vma=False
    )
```

profile of v0, /device:TPU:24, one launch (start us, length us, event | category | flops | bytes accessed | tf_op | source)
XLA Modules:
  0.0 351.3 jit_solution(18037519778036278335)
XLA Ops:
  7.2 0.7 fusion.49
  7.9 1.5 copy.23
  9.4 1.6 gather_fusion
  11.8 0.7 copy-done.8
  12.5 0.7 copy-done.9
  13.1 0.6 fusion.52
  13.7 0.6 fusion.45
  14.4 0.6 fusion.27
  15.7 0.7 multiply_reduce_fusion.2
  16.4 0.7 divide_multiply_fusion.1
  17.0 1.9 fusion.8
  18.9 1.8 fusion.53
  20.7 0.6 multiply_reduce_fusion.6
  21.4 0.7 copy-done.12
  22.0 0.5 rsqrt_multiply_fusion.4
  22.5 0.7 bitcast_subtract_fusion.1
  23.2 1.9 collective-permute-start
  25.1 5.0 %collective-permute-start.1 = (f32[128]{0:T(128)}, f32[128]{0:T(128)}, u32[]{:S(2)}, u32[]{:S(2)}) collective-permute-start(f32[128]{0:T(128)} %get-tuple-element.92), channel_id=1, source_target_pairs={{508,0},{0,4},{4,8},{8,12},{12,16},{16,20},{20,24},{24,28},{28,32}... | collective-permute-start | bytes 1544 | tf_op jit(solution)/shard_map/ppermute | solution.py:13
  30.1 1.3 fusion.14
  31.4 1.8 fusion.55
  33.3 1.6 gather_fusion.1
  35.2 0.7 fusion.46
  35.9 2.5 copy.29
  38.4 0.6 multiply_reduce_fusion.5
  39.0 0.7 copy-done.11
  39.7 4.7 %scatter_custom_fusion = f32[512,400]{1,0:T(8,128)S(1)} fusion(s32[512]{0:T(512)S(1)} %bitcast.81, f32[512,400]{1,0:T(8,128)} %copy.29, f32[]{:T(128)} %constant.39.clone.1), kind=kCustom, calls=%fused_computation.34 | custom fusion | flops 204800 | bytes 819712 | tf_op jit(solution)/shard_map/while/body/eval_jaxpr/scatter-add | solution.py:93
  44.5 0.4 fusion.32
  44.9 1.5 fusion.25
  46.4 0.7 multiply_reduce_fusion.1
  47.1 0.7 divide_multiply_fusion
  47.7 0.6 fusion.10
  48.4 1.9 fusion.9
  50.2 1.8 fusion.56
  52.1 1.8 fusion.54
  53.9 0.6 multiply_reduce_fusion.4
  54.5 0.6 multiply_reduce_fusion.3
  55.2 0.5 copy-done.1
  55.7 1.3 copy.30
  57.0 5.3 %scatter_custom_fusion.1 = f32[512,400]{1,0:T(8,128)} fusion(s32[512]{0:T(512)S(1)} %bitcast.80, f32[512,400]{1,0:T(8,128)} %copy.30, f32[]{:T(128)} %constant.39.clone.1), kind=kCustom, calls=%fused_computation.32 | custom fusion | flops 204800 | bytes 819712 | tf_op jit(solution)/shard_map/while/body/eval_jaxpr/scatter-add | solution.py:93
  62.3 2.5 add.156
  64.7 0.7 subtract_bitcast_fusion
  65.5 0.5 bitcast_add_fusion
  66.0 1.1 fusion.47
  67.1 1.6 subtract_bitcast_fusion.1
  68.7 272.3 %all-reduce.2.cloned.1.call-done = f32[512,400]{1,0:T(8,128)} async-done(((f32[512,400]{1,0:T(8,128)}), f32[512,400]{1,0:T(8,128)}) %all-reduce.2.cloned.1.call-update) | async-done | bytes 819216 | tf_op jit(solution)/shard_map/psum | solution.py:104
  341.0 1.5 multiply_reduce_fusion
  342.5 0.6 rsqrt_multiply_fusion
  343.3 1.2 copy.32
  (38 shorter events, 2.0 us)
Async XLA Ops:
  7.2 333.8 %all-reduce.2.cloned.1.call-start = ((), (), s32[]{:S(2)}) async-start(), calls=%async_computation | async-start | bytes 2097152 | tf_op jit(solution)/shard_map/psum | solution.py:104
  7.9 1.5 copy-start.6
  11.1 0.7 copy-start.7
  11.1 3.3 copy-start.4
  11.8 0.7 copy-start.8
  12.4 0.7 copy-start.9
  14.4 0.9 copy-start.2
  21.4 0.7 copy-start.12
  23.2 21.6 %collective-permute-start = (f32[128,400]{0,1:T(8,128)}, f32[128,400]{0,1:T(8,128)}, u32[]{:S(2)}, u32[]{:S(2)}) collective-permute-start(f32[128,400]{0,1:T(8,128)} %bitcast_subtract_fusion.1), channel_id=1, source_target_pairs={{508,0},{0,4},{4,8},{8,12},{12,16},{16,20},{20,24},{24,28},{28,32}... | collective-permute-start | bytes 614408 | tf_op jit(solution)/shard_map/ppermute | solution.py:13
  25.1 40.8 %collective-permute-start.1 = (f32[128]{0:T(128)}, f32[128]{0:T(128)}, u32[]{:S(2)}, u32[]{:S(2)}) collective-permute-start(f32[128]{0:T(128)} %get-tuple-element.92), channel_id=1, source_target_pairs={{508,0},{0,4},{4,8},{8,12},{12,16},{16,20},{20,24},{24,28},{28,32}... | collective-permute-start | bytes 1544 | tf_op jit(solution)/shard_map/ppermute | solution.py:13
  35.9 2.5 copy-start.5
  38.4 1.3 copy-start.3
  39.0 0.7 copy-start.11
  54.5 1.1 copy-start.1
  68.7 273.8 %copy-start.10 = (f32[512]{0:T(512)S(1)}, f32[512]{0:T(512)}, u32[]{:S(2)}) copy-start(f32[512]{0:T(512)} %param.16) | copy-start | bytes 6148
  341.0 2.1 copy-start
Sparse Core Ops, SparseCore 0:
  64.9 276.0 all-reduce.1
where the time goes:
time: 352 us; the launch traced here: 351 us
  waiting for transfers between devices  272 us (77%)
  other arithmetic  22.6 us (6%)
  matrix products  19.7 us (6%)
  local copies, waits for them, and re-layouts  15.5 us (4%)
  between operations  14.3 us (4%)
  starting transfers between devices  6.93 us (2%)
    psum x1, waiting for transfers between devices, on_device(): total = total + lax.psum(grad_relation, ('blk', 'grp'))  272 us
    scatter-add x2, other arithmetic, visit(): jax.ops.segment_sum(grad_query * left, these_kinds, num_segments=kinds)  10 us
  transfers between devices with their start and end apart: 3, of which 1 were waited for; matrix products, arithmetic and copies ran while one was open for 11% of the time, Pallas kernels for 0%

commit v1 on v0

v1 whole, which is shorter than its diff:
```python
import functools

import jax
import jax.numpy as jnp
import numpy as np
from jax import lax
from jax.experimental import pallas as pl
from jax.experimental.pallas import tpu as pltpu
from jax.sharding import Mesh
from jax.sharding import PartitionSpec as P

learning_rate = 0.1
relation_rate = 0.1

SIZES = (4, 2, 8, 2, 4)
AXES = ("x", "h", "y", "c", "l")
BLK = ("x", "h", "y", "c")
F32 = jnp.float32
VM = pl.BlockSpec(memory_space=pltpu.VMEM)
LANES = 128
TILES = 50
OWNERS = 16
FIRST = [TILES * d // OWNERS for d in range(OWNERS)] + [TILES]


def place(x, h, y, c, l):
    return (((x * 2 + h) * 8 + y) * 2 + c) * 4 + l


def plane_groups():
    first = [[place(x, h, y, 0, l) for x in range(4) for y in range(8)] for h in range(2) for l in range(4)]
    second = [[place(x, h, y, 1, l) for x in range(4) for h in range(2) for l in range(4)] for y in range(8)]
    return first + second


def line_groups():
    first = [[place(x, h, y, 0, l) for h in range(2) for l in range(4)] for x in range(4) for y in range(8)]
    second = [[place(x, h, y, 1, l) for y in range(8)] for x in range(4) for h in range(2) for l in range(4)]
    return first + second


def split(value):
    high = value.astype(jnp.bfloat16)
    return high, (value - high.astype(F32)).astype(jnp.bfloat16)


def product(left, right, dims=((1,), (0,))):
    return lax.dot_general(left, right, (dims, ((), ())), preferred_element_type=F32)


def product3(left, right, dims=((1,), (0,))):
    lh, ll = left
    rh, rl = right
    return product(lh, rh, dims) + product(lh, rl, dims) + product(ll, rh, dims)


def one_hot(ids, count):
    rows = lax.broadcasted_iota(jnp.int32, (count, ids.shape[1]), 0)
    return (rows == ids).astype(F32).astype(jnp.bfloat16)


def gather(table, hot):
    high, low = split(table)
    if high.shape[1] == LANES:
        return product(jnp.concatenate([high, low], 1), jnp.concatenate([hot, hot], 0))
    return product(high, hot) + product(low, hot)


def scatter(values, hot):
    high, low = split(values)
    across = ((1,), (1,))
    return product(high, hot, across) + product(low, hot, across)


def adagrad(weights, accum, grads, rate):
    fresh = accum + jnp.sum(grads * grads, axis=0, keepdims=True) / grads.shape[0]
    return weights - rate * grads * lax.rsqrt(fresh), fresh


def scores(query, right, sampled, count):
    slots, negatives = query.shape[1], sampled.shape[1]
    alive = (lax.broadcasted_iota(jnp.int32, (1, slots), 1) < count).astype(F32)
    positive = jnp.sum(query * right, axis=0, keepdims=True)
    negative = product3(split(sampled.T), split(query))
    pull = -alive * jax.nn.sigmoid(-positive)
    push = jax.nn.sigmoid(negative) * (alive / negatives)
    return pull, push


def target_grads(query, pull, push, target_hot, sample_hot):
    to_samples = product3(split(query), split(push), ((1,), (1,)))
    return scatter(pull * query, target_hot) + scatter(to_samples, sample_hot)


def first_edges(
    source, source_acc, target, relation, sid, tid, kid, nid, cnt,
    moved, query_out, pull_out, push_out, typed_out,
):
    left = gather(source[...], one_hot(sid[0, 0], LANES))
    right = gather(target[...], one_hot(tid[0, 0], LANES))
    sampled = gather(target[...], one_hot(nid[0, 0, 0], LANES))
    scale = gather(relation[...], one_hot(kid[0, 0], relation.shape[1]))
    query = left * scale
    pull, push = scores(query, right, sampled, cnt[0, 0, 0])
    grad_query = pull * right + product3(split(sampled), split(push))
    grads = scatter(grad_query * scale, one_hot(sid[0, 0], LANES))
    rows, acc = adagrad(source[...], source_acc[...], grads, learning_rate)
    width = source.shape[0]
    moved[0:width, :] = rows
    moved[width : width + 8, :] = jnp.broadcast_to(acc, (8, LANES))
    query_out[...] = query
    pull_out[...] = pull
    push_out[...] = push
    typed_out[...] = grad_query * left


def first_rest(
    target, target_acc, relation, tid, kid, nid, query, pull, push, typed,
    target_out, target_acc_out, total, right_out, sampled_out, scale_out,
):
    grads = target_grads(
        query[...], pull[...], push[...], one_hot(tid[0, 0], LANES), one_hot(nid[0, 0, 0], LANES)
    )
    rows, acc = adagrad(target[...], target_acc[...], grads, learning_rate)
    target_out[...] = rows
    target_acc_out[...] = acc
    sums = scatter(typed[...], one_hot(kid[0, 0], relation.shape[1]))
    half = sums.shape[1] // 2
    total[0] = sums[:, :half]
    total[1] = sums[:, half:]
    right_out[...] = gather(rows, one_hot(tid[1, 0], LANES))
    sampled_out[...] = gather(rows, one_hot(nid[1, 0, 0], LANES))
    scale_out[...] = gather(relation[...], one_hot(kid[1, 0], relation.shape[1]))


def put_blocks(out, sums):
    for block in range(2):
        lanes = slice(block * LANES, (block + 1) * LANES)
        for d in range(OWNERS):
            row = FIRST[d] * 8
            out[block * OWNERS + d] = sums[row : row + 32, lanes]


def second_edges(
    moved, right, sampled, scale, sid, kid, cnt, total,
    query_out, pull_out, push_out, grad_out, typed_out, sent,
):
    width = right.shape[0]
    left = gather(moved[0:width, :], one_hot(sid[1, 0], LANES))
    query = left * scale[...]
    pull, push = scores(query, right[...], sampled[...], cnt[1, 0, 0])
    grad_query = pull * right[...] + product3(split(sampled[...]), split(push))
    typed = grad_query * left
    other = 1 - lax.axis_index("c")
    half = total.shape[2]
    put_blocks(sent, total[other] + scatter(typed, one_hot(kid[1, 0] - other * half, half)))
    query_out[...] = query
    pull_out[...] = pull
    push_out[...] = push
    grad_out[...] = grad_query
    typed_out[...] = typed


def second_rest(
    moved, target, target_acc, scale, sid, tid, kid, nid, query, pull, push, grad_query, typed, total,
    source_out, source_acc_out, target_out, target_acc_out, kept,
):
    width = target.shape[0]
    me = lax.axis_index("c")
    half = total.shape[2]
    put_blocks(kept, total[me] + scatter(typed[...], one_hot(kid[1, 0] - me * half, half)))
    grads = target_grads(
        query[...], pull[...], push[...], one_hot(tid[1, 0], LANES), one_hot(nid[1, 0, 0], LANES)
    )
    target_out[...], target_acc_out[...] = adagrad(target[...], target_acc[...], grads, learning_rate)
    grads = scatter(grad_query[...] * scale[...], one_hot(sid[1, 0], LANES))
    source_out[...], source_acc_out[...] = adagrad(
        moved[0:width, :], moved[width : width + 1, :], grads, learning_rate
    )


def last_update(mine, theirs, relation, relation_acc, relation_out, relation_acc_out):
    me = lax.axis_index("c")
    for blocks, half in ((mine, me), (theirs, 1 - me)):
        for block in range(2):
            lanes = pl.ds(pl.multiple_of((half * 2 + block) * LANES, LANES), LANES)
            pieces = [
                blocks[block * OWNERS + d, 0 : (FIRST[d + 1] - FIRST[d]) * 8, :] for d in range(OWNERS)
            ]
            grads = jnp.concatenate(pieces, 0)
            relation_out[:, lanes], relation_acc_out[:, lanes] = adagrad(
                relation[:, lanes], relation_acc[:, lanes], grads, relation_rate
            )


def call(kernel, shapes, *operands, flops=0):
    moved = sum(4 * int(np.prod(s)) for s in shapes) + sum(4 * o.size for o in operands)
    return pl.pallas_call(
        kernel,
        out_shape=[jax.ShapeDtypeStruct(s, F32) for s in shapes],
        in_specs=[VM] * len(operands),
        out_specs=[VM] * len(shapes),
        compiler_params=pltpu.CompilerParams(vmem_limit_bytes=40 * 2**20),
        cost_estimate=pl.CostEstimate(flops=flops, bytes_accessed=moved, transcendentals=0),
    )(*operands)


def exchange(blocks, groups):
    return lax.all_to_all(blocks, AXES, 0, 0, axis_index_groups=groups, tiled=True)


def spread(block, count):
    return jnp.broadcast_to(block[None], (count,) + block.shape)


def swap_cores(value):
    return lax.ppermute(value, "c", [(0, 1), (1, 0)])


def on_device(
    source_emb, source_state, target_emb, target_state, relation_emb, relation_state,
    sid, tid, kid, cnt, nid,
):
    source, target, relation = source_emb[0].T, target_emb[0].T, relation_emb.T
    width, kinds = relation.shape
    slots, negatives = sid.shape[-1], nid.shape[-1]
    table, row = (width, LANES), (1, LANES)
    edges, pairs = (width, slots), (negatives, slots)
    blocks = (2 * OWNERS, 32, LANES)
    work = 10**9
    moved, query, pull, push, typed = call(
        first_edges, [(width + 8, LANES), edges, (1, slots), pairs, edges],
        source, source_state, target, relation, sid, tid, kid, nid, cnt, flops=2 * work,
    )
    count = lax.axis_size(BLK)
    moved = lax.ppermute(moved, BLK, [(i, (i + 1) % count) for i in range(count)])
    target, target_acc, total, right, sampled, scale = call(
        first_rest, [table, row, (2, width, kinds // 2), edges, (width, negatives), edges],
        target, target_state, relation, tid, kid, nid, query, pull, push, typed, flops=2 * work,
    )
    query, pull, push, grad_query, typed, sent = call(
        second_edges, [edges, (1, slots), pairs, edges, edges, blocks],
        moved, right, sampled, scale, sid, kid, cnt, total, flops=2 * work,
    )
    received = swap_cores(sent)
    source, source_acc, target, target_acc, kept = call(
        second_rest, [table, row, table, row, blocks],
        moved, target, target_acc, scale, sid, tid, kid, nid, query, pull, push, grad_query, typed, total,
        flops=2 * work,
    )
    planes, lines = plane_groups(), line_groups()
    block = jnp.sum(exchange(kept + received, planes), 0)
    block = jnp.sum(exchange(spread(block, 8), lines), 0)
    mine = exchange(spread(block, 2 * OWNERS), planes)
    theirs = swap_cores(mine)
    relation, relation_acc = call(
        last_update, [(width, kinds), (1, kinds)], mine, theirs, relation, relation_state[None]
    )
    return (source.T[None], source_acc, target.T[None], target_acc, relation.T, relation_acc[0])


def solution(mesh):
    fine = Mesh(mesh.devices.reshape(SIZES), AXES)
    slab, sums = P(BLK, "l", None), P(BLK, "l")
    ids = P(None, BLK, "l", None)
    in_specs = (
        slab, sums, slab, sums, P(), P(), ids, ids, ids, P(None, BLK, "l"), P(None, BLK, "l", None, None),
    )
    out_specs = (slab, sums, slab, sums, P(), P())
    return jax.shard_map(
        on_device, mesh=fine, in_specs=in_specs, out_specs=out_specs, check_vma=False
    )
```

time: 352 us -> 91.5 us (0.26)
  the two profiles are of different devices: /device:TPU:24 before, /device:TPU:9 now
where the time goes in v1:
time: 91.5 us; the launch traced here: 91 us
  blocking collectives  58.6 us (64%)
  starting transfers between devices  13.8 us (15%)
  Pallas kernels  9.62 us (11%)
  local copies, waits for them, and re-layouts  6.51 us (7%)
  waiting for transfers between devices  1.52 us (2%)
    all_to_all x3, blocking collectives, exchange(): lax.all_to_all(blocks, AXES, 0, 0, axis_index_groups=groups, tiled=True)  58.6 us
    ppermute x2, starting transfers between devices, swap_cores(): return lax.ppermute(value, 'c', [(0, 1), (1, 0)])  10.1 us
    pallas_call x5, Pallas kernels, call(): pl.pallas_call(kernel, out_shape=[jax.ShapeDtypeStruct(s, F32) for s in s...  9.62 us
    unnamed x27, local copies, waits for them, and re-layouts  6.45 us
    ppermute x1, starting transfers between devices, on_device(): lax.ppermute(moved, BLK, [(i, (i + 1) % count) for i in range(count)])  3.76 us
  transfers between devices with their start and end apart: 3, of which 1 were waited for; matrix products, arithmetic and copies ran while one was open for 0% of the time, Pallas kernels for 5%

profile of v1, /device:TPU:9, one launch (start us, length us, event | category | flops | bytes accessed | tf_op | source)
XLA Modules:
  0.0 91.0 jit_solution(17655233024237713162)
XLA Ops:
  0.6 0.0 copy-start.5
  0.6 0.7 copy.19.cnt
  1.4 0.0 copy-start.10
  1.4 0.0 copy-start.11
  1.4 0.0 copy-done.5
  1.4 0.7 copy-done.10
  2.1 0.0 copy-done.11
  2.1 0.0 copy-start
  2.1 1.1 %copy-done = f32[512,400]{0,1:T(8,128)S(1)} copy-done((f32[512,400]{0,1:T(8,128)S(1)}, f32[512,400]{0,1:T(8,128)}, u32[]{:S(2)}) %copy-start) | copy-done | bytes 819224
  3.2 0.0 copy-start.3
  3.2 0.9 %copy-done.3 = f32[1,128,400]{1,2,0:T(8,128)S(1)} copy-done((f32[1,128,400]{1,2,0:T(8,128)S(1)}, f32[1,128,400]{1,2,0:T(8,128)}, u32[]{:S(2)}) %copy-start.3) | copy-done | bytes 204824
  4.2 0.0 copy-start.4
  4.2 0.9 %copy-done.4 = f32[1,128,400]{1,2,0:T(8,128)S(1)} copy-done((f32[1,128,400]{1,2,0:T(8,128)S(1)}, f32[1,128,400]{1,2,0:T(8,128)}, u32[]{:S(2)}) %copy-start.4) | copy-done | bytes 204824
  5.1 0.0 copy-start.6
  5.1 0.7 copy-done.6
  5.8 0.0 copy-start.8
  5.8 0.7 copy-done.8
  6.5 0.0 copy-start.1
  6.5 2.5 %shard_map.154 = (f32[408,128]{1,0:T(8,128)S(1)}, f32[400,512]{1,0:T(8,128)S(1)}, f32[1,512]{1,0:T(1,128)S(1)}, f32[256,512]{1,0:T(8,128)S(1)}, f32[400,512]{1,0:T(8,128)S(1)}) custom-call(f32[400,128]{1,0:T(8,128)S(1)} %bitcast.20, f32[1,128]{1,0:T(1,128)S(1)} %copy-done.11, f32[400,128]{1,0:T(8,128)S(1)} %bitcast.21, f32[400,512]{1,0:T(8,128)S(1)} %bitcast.16, ...), custom_call_target="tpu_custom_call" | custom-call | flops 2000000000 | bytes 3617288 | tf_op jit(solution)/shard_map/pallas_call | solution.py:198
  9.0 0.0 copy-start.9
  9.0 0.0 copy-start.7
  9.0 3.8 %collective-permute-start = (f32[408,128]{1,0:T(8,128)S(1)}, f32[408,128]{1,0:T(8,128)S(1)}, u32[]{:S(2)}, u32[]{:S(2)}) collective-permute-start(f32[408,128]{1,0:T(8,128)S(1)} %get-tuple-element.30), channel_id=1, source_target_pairs={{0,4},{4,8},{8,12},{12,16},{16,20},{20,24},{24,28},{28,32},{32,36}... | collective-permute-start | bytes 626696 | tf_op jit(solution)/shard_map/ppermute | solution.py:236
  12.8 0.0 copy-start.12
  12.8 0.0 copy-done.1
  12.8 0.0 copy-done.9
  12.8 0.0 copy-done.7
  12.8 0.6 copy-done.12
  13.4 2.2 %shard_map.155 = (f32[400,128]{1,0:T(8,128)S(1)}, f32[1,128]{1,0:T(1,128)S(1)}, f32[2,400,256]{2,1,0:T(8,128)S(1)}, f32[400,512]{1,0:T(8,128)S(1)}, f32[400,256]{1,0:T(8,128)S(1)}, /*index=5*/f32[400,512]{1,0:T(8,128)S(1)}) custom-call(f32[400,128]{1,0:T(8,128)S(1)} %bitcast.22, f32[1,128]{1,0:T(1,128)S(1)} %copy-done.12, f32[400,512]{1,0:T(8,128)S(1)} %bitcast.17, ...), custom_call_target="tpu_custom_call" | custom-call | flops 2000000000 | bytes 6272000 | tf_op jit(solution)/shard_map/pallas_call | solution.py:198
  15.6 0.0 collective-permute-done.moved
  15.6 1.7 %shard_map.156 = (f32[400,512]{1,0:T(8,128)S(1)}, f32[1,512]{1,0:T(1,128)S(1)}, f32[256,512]{1,0:T(8,128)S(1)}, f32[400,512]{1,0:T(8,128)S(1)}, f32[400,512]{1,0:T(8,128)S(1)}, /*index=5*/f32[32,32,128]{2,1,0:T(8,128)S(1)}) custom-call(f32[408,128]{1,0:T(8,128)S(1)} %collective-permute-done.moved, f32[400,512]{1,0:T(8,128)S(1)} %get-tuple-element.38.right, ...), custom_call_target="tpu_custom_call" | custom-call | flops 2000000000 | bytes 6592520 | tf_op jit(solution)/shard_map/pallas_call | solution.py:198
  17.3 3.1 %collective-permute-start.1 = (f32[32,32,128]{2,1,0:T(8,128)S(1)}, f32[32,32,128]{2,1,0:T(8,128)S(1)}, u32[]{:S(2)}, u32[]{:S(2)}) collective-permute-start(f32[32,32,128]{2,1,0:T(8,128)S(1)} %get-tuple-element.51), channel_id=1, source_target_pairs={{0,4},{4,0},{1,5},{5,1},{2,6},{6,2},{3,7},{7,3},{8,12},{12,8},{9,1... | collective-permute-start | bytes 1572872 | tf_op jit(solution)/shard_map/ppermute | solution.py:217
  20.4 2.1 %shard_map.157 = (f32[400,128]{1,0:T(8,128)}, f32[1,128]{1,0:T(1,128)}, f32[400,128]{1,0:T(8,128)}, f32[1,128]{1,0:T(1,128)}, f32[32,32,128]{2,1,0:T(8,128)S(1)}) custom-call(f32[408,128]{1,0:T(8,128)S(1)} %collective-permute-done.moved, f32[400,128]{1,0:T(8,128)S(1)} %get-tuple-element.35.target, f32[1,128]{1,0:T(1,128)S(1)} %get-tuple-element.36.target_acc, ...), custom_call_target="tpu_custom_call" | custom-call | flops 2000000000 | bytes 5985792 | tf_op jit(solution)/shard_map/pallas_call | solution.py:198
  22.5 0.0 collective-permute-done.1
  22.5 0.1 add.3
  22.6 24.4 %all_to_all.15 = f32[32,32,128]{2,1,0:T(8,128)S(1)} all-to-all(f32[32,32,128]{2,1,0:T(8,128)S(1)} %add.3), channel_id=1, replica_groups={{0,8,16,24,32,40,48,56,128,136,144,152,160,168,176,184,256,264,272,280,..., dimensions={0} | all-to-all | bytes 1048576 | tf_op jit(solution)/shard_map/all_to_all | solution.py:209
  47.1 17.2 %all_to_all.16 = f32[8,32,128]{2,1,0:T(8,128)S(1)} all-to-all(f32[8,32,128]{2,1,0:T(8,128)S(1)} %broadcast_in_dim.23), channel_id=1, replica_groups={{0,1,2,3,64,65,66,67},{8,9,10,11,72,73,74,75},{16,17,18,19,80,81,82,83}..., dimensions={0} | all-to-all | bytes 262144 | tf_op jit(solution)/shard_map/all_to_all | solution.py:209
  64.3 0.1 broadcast_in_dim.24
  64.4 0.0 copy-start.2
  64.4 17.0 %all_to_all.17.mine = f32[32,32,128]{2,1,0:T(8,128)S(1)} all-to-all(f32[32,32,128]{2,1,0:T(8,128)S(1)} %broadcast_in_dim.24), channel_id=1, replica_groups={{0,8,16,24,32,40,48,56,128,136,144,152,160,168,176,184,256,264,272,280,..., dimensions={0} | all-to-all | bytes 1048576 | tf_op jit(solution)/shard_map/all_to_all | solution.py:209
  81.3 7.0 %collective-permute-start.2 = (f32[32,32,128]{2,1,0:T(8,128)S(1)}, f32[32,32,128]{2,1,0:T(8,128)S(1)}, u32[]{:S(2)}, u32[]{:S(2)}) collective-permute-start(f32[32,32,128]{2,1,0:T(8,128)S(1)} %all_to_all.17.mine), channel_id=1, source_target_pairs={{0,4},{4,0},{1,5},{5,1},{2,6},{6,2},{3,7},{7,3},{8,12},{12,8},{9,1... | collective-permute-start | bytes 1572872 | tf_op jit(solution)/shard_map/ppermute | solution.py:217
  88.3 1.5 %collective-permute-done.2.theirs = f32[32,32,128]{2,1,0:T(8,128)S(1)} collective-permute-done((f32[32,32,128]{2,1,0:T(8,128)S(1)}, f32[32,32,128]{2,1,0:T(8,128)S(1)}, u32[]{:S(2)}, u32[]{:S(2)}) %collective-permute-start.2) | collective-permute-done | bytes 524320 | tf_op jit(solution)/shard_map/ppermute | solution.py:217
  89.8 0.0 copy-done.2
  89.8 1.1 %shard_map.158 = (f32[400,512]{1,0:T(8,128)}, f32[1,512]{1,0:T(1,128)}) custom-call(f32[32,32,128]{2,1,0:T(8,128)S(1)} %all_to_all.17.mine, f32[32,32,128]{2,1,0:T(8,128)S(1)} %collective-permute-done.2.theirs, f32[400,512]{1,0:T(8,128)S(1)} %bitcast.18, f32[1,512]{1,0:T(1,128)S(1)} %bitcast.19), custom_call_target="tpu_custom_call" | custom-call | bytes 2691072 | tf_op jit(solution)/shard_map/pallas_call | solution.py:198
  (3 shorter events, 0.1 us)
Async XLA Ops:
  0.6 0.8 copy-start.5
  1.4 0.7 copy-start.10
  1.4 0.7 copy-start.11
  2.1 1.1 %copy-start = (f32[512,400]{0,1:T(8,128)S(1)}, f32[512,400]{0,1:T(8,128)}, u32[]{:S(2)}) copy-start(f32[512,400]{0,1:T(8,128)} %param.15) | copy-start | bytes 2457604
  3.2 0.9 %copy-start.3 = (f32[1,128,400]{1,2,0:T(8,128)S(1)}, f32[1,128,400]{1,2,0:T(8,128)}, u32[]{:S(2)}) copy-start(f32[1,128,400]{1,2,0:T(8,128)} %param.11) | copy-start | bytes 614404
  4.2 0.9 %copy-start.4 = (f32[1,128,400]{1,2,0:T(8,128)S(1)}, f32[1,128,400]{1,2,0:T(8,128)}, u32[]{:S(2)}) copy-start(f32[1,128,400]{1,2,0:T(8,128)} %param.13) | copy-start | bytes 614404
  5.1 0.7 copy-start.6
  5.8 0.7 copy-start.8
  6.5 6.3 %copy-start.1 = (f32[512,400]{0,1:T(8,128)S(1)}, f32[512,400]{0,1:T(8,128)}, u32[]{:S(2)}) copy-start(f32[512,400]{0,1:T(8,128)} %param.15) | copy-start | bytes 2457604
  9.0 3.8 %copy-start.9 = (s32[2,1,1,512]{3,2,1,0:T(1,128)S(1)}, s32[2,1,1,512]{3,2,1,0:T(1,128)}, u32[]{:S(2)}) copy-start(s32[2,1,1,512]{3,2,1,0:T(1,128)} %kid.7) | copy-start | bytes 12292
  9.0 3.8 %copy-start.7 = (s32[2,1,1,512]{3,2,1,0:T(1,128)S(1)}, s32[2,1,1,512]{3,2,1,0:T(1,128)}, u32[]{:S(2)}) copy-start(s32[2,1,1,512]{3,2,1,0:T(1,128)} %tid.5) | copy-start | bytes 12292
  9.0 6.6 %collective-permute-start = (f32[408,128]{1,0:T(8,128)S(1)}, f32[408,128]{1,0:T(8,128)S(1)}, u32[]{:S(2)}, u32[]{:S(2)}) collective-permute-start(f32[408,128]{1,0:T(8,128)S(1)} %get-tuple-element.30), channel_id=1, source_target_pairs={{0,4},{4,8},{8,12},{12,16},{16,20},{20,24},{24,28},{28,32},{32,36}... | collective-permute-start | bytes 626696 | tf_op jit(solution)/shard_map/ppermute | solution.py:236
  12.8 0.7 copy-start.12
  17.3 5.2 %collective-permute-start.1 = (f32[32,32,128]{2,1,0:T(8,128)S(1)}, f32[32,32,128]{2,1,0:T(8,128)S(1)}, u32[]{:S(2)}, u32[]{:S(2)}) collective-permute-start(f32[32,32,128]{2,1,0:T(8,128)S(1)} %get-tuple-element.51), channel_id=1, source_target_pairs={{0,4},{4,0},{1,5},{5,1},{2,6},{6,2},{3,7},{7,3},{8,12},{12,8},{9,1... | collective-permute-start | bytes 1572872 | tf_op jit(solution)/shard_map/ppermute | solution.py:217
  64.4 25.5 %copy-start.2 = (f32[512]{0:T(512)S(1)}, f32[512]{0:T(512)}, u32[]{:S(2)}) copy-start(f32[512]{0:T(512)} %param.16) | copy-start | bytes 6148
  81.3 8.5 %collective-permute-start.2 = (f32[32,32,128]{2,1,0:T(8,128)S(1)}, f32[32,32,128]{2,1,0:T(8,128)S(1)}, u32[]{:S(2)}, u32[]{:S(2)}) collective-permute-start(f32[32,32,128]{2,1,0:T(8,128)S(1)} %all_to_all.17.mine), channel_id=1, source_target_pairs={{0,4},{4,0},{1,5},{5,1},{2,6},{6,2},{3,7},{7,3},{8,12},{12,8},{9,1... | collective-permute-start | bytes 1572872 | tf_op jit(solution)/shard_map/ppermute | solution.py:217

commit v2 on v1

--- a/solution.py
+++ b/solution.py
@@ -1,5 +1,3 @@
-import functools
-
 import jax
 import jax.numpy as jnp
 import numpy as np
@@ -18,9 +16,6 @@
 F32 = jnp.float32
 VM = pl.BlockSpec(memory_space=pltpu.VMEM)
 LANES = 128
-TILES = 50
-OWNERS = 16
-FIRST = [TILES * d // OWNERS for d in range(OWNERS)] + [TILES]
 
 
 def place(x, h, y, c, l):
@@ -92,39 +87,57 @@
     return scatter(pull * query, target_hot) + scatter(to_samples, sample_hot)
 
 
-def first_edges(
-    source, source_acc, target, relation, sid, tid, kid, nid, cnt,
-    moved, query_out, pull_out, push_out, typed_out,
-):
-    left = gather(source[...], one_hot(sid[0, 0], LANES))
-    right = gather(target[...], one_hot(tid[0, 0], LANES))
-    sampled = gather(target[...], one_hot(nid[0, 0, 0], LANES))
-    scale = gather(relation[...], one_hot(kid[0, 0], relation.shape[1]))
+def bucket(source, target, scale, sid, tid, nid, cnt):
+    left = gather(source, one_hot(sid, LANES))
+    right = gather(target, one_hot(tid, LANES))
+    sampled = gather(target, one_hot(nid, LANES))
     query = left * scale
-    pull, push = scores(query, right, sampled, cnt[0, 0, 0])
+    pull, push = scores(query, right, sampled, cnt)
     grad_query = pull * right + product3(split(sampled), split(push))
+    return left, query, pull, push, grad_query
+
+
+def first_source(
+    kid_in, relation_in, sid_in, source_in, tid_in, target_in, nid_in, cnt_in, source_acc_in, moved,
+    kid, relation, sid, source, tid, target, nid, cnt, source_acc, arrived,
+):
+    wanted = (
+        (kid_in, kid), (relation_in, relation), (sid_in, sid), (source_in, source), (tid_in, tid),
+        (target_in, target), (nid_in, nid), (cnt_in, cnt), (source_acc_in, source_acc),
+    )
+    copies = [pltpu.make_async_copy(a, b, arrived.at[i]) for i, (a, b) in enumerate(wanted)]
+    for copy in copies:
+        copy.start()
+    copies[0].wait()
+    kind_hot = one_hot(kid[0, 0], relation.shape[1])
+    copies[1].wait()
+    scale = gather(relation[...], kind_hot)
+    for copy in copies[2:]:
+        copy.wait()
+    grad_query = bucket(
+        source[...], target[...], scale, sid[0, 0], tid[0, 0], nid[0, 0, 0], cnt[0, :, 0:1]
+    )[-1]
     grads = scatter(grad_query * scale, one_hot(sid[0, 0], LANES))
     rows, acc = adagrad(source[...], source_acc[...], grads, learning_rate)
     width = source.shape[0]
     moved[0:width, :] = rows
     moved[width : width + 8, :] = jnp.broadcast_to(acc, (8, LANES))
-    query_out[...] = query
-    pull_out[...] = pull
-    push_out[...] = push
-    typed_out[...] = grad_query * left
 
 
 def first_rest(
-    target, target_acc, relation, tid, kid, nid, query, pull, push, typed,
+    source, target, target_acc, relation, sid, tid, kid, nid, cnt,
     target_out, target_acc_out, total, right_out, sampled_out, scale_out,
 ):
-    grads = target_grads(
-        query[...], pull[...], push[...], one_hot(tid[0, 0], LANES), one_hot(nid[0, 0, 0], LANES)
-    )
+    kind_hot = one_hot(kid[0, 0], relation.shape[1])
+    left, query, pull, push, grad_query = bucket(
+        source[...], target[...], gather(relation[...], kind_hot), sid[0, 0], tid[0, 0], nid[0, 0, 0],
+        cnt[0, :, 0:1],
+    )
+    grads = target_grads(query, pull, push, one_hot(tid[0, 0], LANES), one_hot(nid[0, 0, 0], LANES))
     rows, acc = adagrad(target[...], target_acc[...], grads, learning_rate)
     target_out[...] = rows
     target_acc_out[...] = acc
-    sums = scatter(typed[...], one_hot(kid[0, 0], relation.shape[1]))
+    sums = scatter(grad_query * left, kind_hot)
     half = sums.shape[1] // 2
     total[0] = sums[:, :half]
     total[1] = sums[:, half:]
@@ -134,11 +147,9 @@
 
 
 def put_blocks(out, sums):
-    for block in range(2):
-        lanes = slice(block * LANES, (block + 1) * LANES)
-        for d in range(OWNERS):
-            row = FIRST[d] * 8
-            out[block * OWNERS + d] = sums[row : row + 32, lanes]
+    width = sums.shape[0]
+    for block in range(sums.shape[1] // LANES):
+        out[block * width : (block + 1) * width, :] = sums[:, block * LANES : (block + 1) * LANES]
 
 
 def second_edges(
@@ -148,7 +159,7 @@
     width = right.shape[0]
     left = gather(moved[0:width, :], one_hot(sid[1, 0], LANES))
     query = left * scale[...]
-    pull, push = scores(query, right[...], sampled[...], cnt[1, 0, 0])
+    pull, push = scores(query, right[...], sampled[...], cnt[0, :, 1:2])
     grad_query = pull * right[...] + product3(split(sampled[...]), split(push))
     typed = grad_query * left
     other = 1 - lax.axis_index("c")
@@ -179,28 +190,28 @@
     )
 
 
-def last_update(mine, theirs, relation, relation_acc, relation_out, relation_acc_out):
-    me = lax.axis_index("c")
-    for blocks, half in ((mine, me), (theirs, 1 - me)):
-        for block in range(2):
-            lanes = pl.ds(pl.multiple_of((half * 2 + block) * LANES, LANES), LANES)
-            pieces = [
-                blocks[block * OWNERS + d, 0 : (FIRST[d + 1] - FIRST[d]) * 8, :] for d in range(OWNERS)
-            ]
-            grads = jnp.concatenate(pieces, 0)
-            relation_out[:, lanes], relation_acc_out[:, lanes] = adagrad(
-                relation[:, lanes], relation_acc[:, lanes], grads, relation_rate
-            )
-
-
-def call(kernel, shapes, *operands, flops=0):
+def last_update(sums, relation, relation_acc, relation_out, relation_acc_out):
+    width, kinds = relation.shape
+    for block in range(kinds // LANES):
+        lanes = slice(block * LANES, (block + 1) * LANES)
+        relation_out[:, lanes], relation_acc_out[:, lanes] = adagrad(
+            relation[:, lanes], relation_acc[:, lanes], sums[block * width : (block + 1) * width, :], relation_rate
+        )
+
+
+def call(kernel, shapes, *operands, flops=0, fetch=False):
+    scratch = []
+    if fetch:
+        scratch = [pltpu.VMEM(o.shape, o.dtype) for o in operands]
+        scratch.append(pltpu.SemaphoreType.DMA((len(operands),)))
     moved = sum(4 * int(np.prod(s)) for s in shapes) + sum(4 * o.size for o in operands)
     return pl.pallas_call(
         kernel,
         out_shape=[jax.ShapeDtypeStruct(s, F32) for s in shapes],
-        in_specs=[VM] * len(operands),
+        in_specs=[pl.BlockSpec(memory_space=pltpu.HBM) if fetch else VM] * len(operands),
         out_specs=[VM] * len(shapes),
-        compiler_params=pltpu.CompilerParams(vmem_limit_bytes=40 * 2**20),
+        scratch_shapes=scratch,
+        compiler_params=pltpu.CompilerParams(vmem_limit_bytes=(60 if fetch else 40) * 2**20),
         cost_estimate=pl.CostEstimate(flops=flops, bytes_accessed=moved, transcendentals=0),
     )(*operands)
 
@@ -222,21 +233,22 @@
     sid, tid, kid, cnt, nid,
 ):
     source, target, relation = source_emb[0].T, target_emb[0].T, relation_emb.T
+    cnt = cnt.transpose(1, 2, 0)
     width, kinds = relation.shape
     slots, negatives = sid.shape[-1], nid.shape[-1]
     table, row = (width, LANES), (1, LANES)
     edges, pairs = (width, slots), (negatives, slots)
-    blocks = (2 * OWNERS, 32, LANES)
+    blocks = (width * kinds // 2 // LANES, LANES)
     work = 10**9
-    moved, query, pull, push, typed = call(
-        first_edges, [(width + 8, LANES), edges, (1, slots), pairs, edges],
-        source, source_state, target, relation, sid, tid, kid, nid, cnt, flops=2 * work,
+    (moved,) = call(
+        first_source, [(width + 8, LANES)],
+        kid, relation, sid, source, tid, target, nid, cnt, source_state, flops=2 * work, fetch=True,
     )
     count = lax.axis_size(BLK)
     moved = lax.ppermute(moved, BLK, [(i, (i + 1) % count) for i in range(count)])
     target, target_acc, total, right, sampled, scale = call(
         first_rest, [table, row, (2, width, kinds // 2), edges, (width, negatives), edges],
-        target, target_state, relation, tid, kid, nid, query, pull, push, typed, flops=2 * work,
+        source, target, target_state, relation, sid, tid, kid, nid, cnt, flops=4 * work,
     )
     query, pull, push, grad_query, typed, sent = call(
         second_edges, [edges, (1, slots), pairs, edges, edges, blocks],
@@ -249,12 +261,13 @@
         flops=2 * work,
     )
     planes, lines = plane_groups(), line_groups()
-    block = jnp.sum(exchange(kept + received, planes), 0)
-    block = jnp.sum(exchange(spread(block, 8), lines), 0)
-    mine = exchange(spread(block, 2 * OWNERS), planes)
-    theirs = swap_cores(mine)
+    in_plane, in_line = len(planes[0]), len(lines[0])
+    block = jnp.sum(exchange((kept + received).reshape(in_plane, 1, -1), planes), 0)
+    block = jnp.sum(exchange(spread(block, in_line), lines), 0)
+    halves = exchange(spread(block, in_plane), planes).reshape(blocks)
+    sums = lax.all_gather(halves, "c", tiled=True)
     relation, relation_acc = call(
-        last_update, [(width, kinds), (1, kinds)], mine, theirs, relation, relation_state[None]
+        last_update, [(width, kinds), (1, kinds)], sums, relation, relation_state[None]
     )
     return (source.T[None], source_acc, target.T[None], target_acc, relation.T, relation_acc[0])
 

time: 91.5 us -> 85 us (0.929)
  starting transfers between devices: 13.8 us -> 5.75 us
  local copies, waits for them, and re-layouts: 6.51 us -> 0.31 us
  blocking collectives: 58.6 us -> 63.3 us
  Pallas kernels: 9.62 us -> 14.1 us
  waiting for transfers between devices: 1.52 us -> 0.01 us
    ppermute x2 -> x1, starting transfers between devices: 10.1 us -> 1.98 us  [swap_cores(): return lax.ppermute(value, 'c', [(0, 1), (1, 0)])]
    all_gather x0 -> x1, blocking collectives: none -> 7.34 us  [on_device(): sums = lax.all_gather(halves, 'c', tiled=True)]
    unnamed x27 -> x20, local copies, waits for them, and re-layouts: 6.45 us -> 0.04 us
    pallas_call x5, Pallas kernels: 9.62 us -> 14.1 us  [call(): pl.pallas_call(kernel, out_shape=[jax.ShapeDtypeStruct(s, F32) for s in s...]
    all_to_all x3, blocking collectives: 58.6 us -> 56 us  [exchange(): lax.all_to_all(blocks, AXES, 0, 0, axis_index_groups=groups, tiled=True)]
    ppermute x2 -> x1, waiting for transfers between devices: 1.52 us -> 0.01 us  [swap_cores(): return lax.ppermute(value, 'c', [(0, 1), (1, 0)])]
  transfers between devices with their start and end apart: 3 -> 2, of which waited for: 1 -> 0; matrix products, arithmetic and copies ran while one was open for 0% -> 0% of each run, Pallas kernels for 5% -> 7%
where the time goes in v2:
time: 85 us; the launch traced here: 84.7 us
  blocking collectives  63.3 us (74%)
  Pallas kernels  14.1 us (17%)
  starting transfers between devices  5.75 us (7%)
  between operations  0.86 us (1%)
    all_to_all x3, blocking collectives, exchange(): lax.all_to_all(blocks, AXES, 0, 0, axis_index_groups=groups, tiled=True)  56 us
    pallas_call x5, Pallas kernels, call(): pl.pallas_call(kernel, out_shape=[jax.ShapeDtypeStruct(s, F32) for s in s...  14.1 us
    all_gather x1, blocking collectives, on_device(): sums = lax.all_gather(halves, 'c', tiled=True)  7.34 us
    ppermute x1, starting transfers between devices, on_device(): lax.ppermute(moved, BLK, [(i, (i + 1) % count) for i in range(count)])  3.77 us
    ppermute x1, starting transfers between devices, swap_cores(): return lax.ppermute(value, 'c', [(0, 1), (1, 0)])  1.98 us
  transfers between devices with their start and end apart: 2, of which 0 were waited for; matrix products, arithmetic and copies ran while one was open for 0% of the time, Pallas kernels for 7%

profile of v2, /device:TPU:9, one launch (start us, length us, event | category | flops | bytes accessed | tf_op | source)
XLA Modules:
  0.0 84.7 jit_solution(17820976960066924707)
XLA Ops:
  0.6 0.0 copy-start
  0.6 0.0 copy-start.2
  0.7 0.0 copy-start.3
  0.7 0.0 copy-start.4
  0.7 0.0 copy-start.5
  0.7 0.0 copy-start.6
  0.7 0.0 copy-start.7
  0.7 0.0 copy-start.8
  0.7 0.0 copy-start.9
  0.7 4.9 %shard_map.154 = f32[408,128]{1,0:T(8,128)} custom-call(s32[2,1,1,512]{3,2,1,0:T(1,128)} %kid.5, f32[400,512]{1,0:T(8,128)} %bitcast.19, s32[2,1,1,512]{3,2,1,0:T(1,128)} %sid.5, f32[400,128]{1,0:T(8,128)} %bitcast.23, s32[2,1,1,512]{3,2,1,0:T(1,128)} %tid.3, f32[400,128]{1,0:T(8,128)} %bitcast.25, s32[2,1,1,1,256]{4,3,2,1,0:T(1,128)} %nid.3, ...), custom_call_target="tpu_custom_call" | custom-call | flops 2000000000 | bytes 1452552 | tf_op jit(solution)/shard_map/pallas_call | solution.py:208
  5.7 3.8 %collective-permute-start = (f32[408,128]{1,0:T(8,128)}, f32[408,128]{1,0:T(8,128)S(1)}, u32[]{:S(2)}, u32[]{:S(2)}) collective-permute-start(f32[408,128]{1,0:T(8,128)} %shard_map.154), channel_id=1, source_target_pairs={{0,4},{4,8},{8,12},{12,16},{16,20},{20,24},{24,28},{28,32},{32,36}... | collective-permute-start | bytes 626696 | tf_op jit(solution)/shard_map/ppermute | solution.py:248
  9.4 0.0 copy-done
  9.5 0.0 copy-done.2
  9.5 0.0 copy-done.3
  9.5 0.0 copy-done.4
  9.5 0.0 copy-done.5
  9.5 0.0 copy-done.6
  9.5 0.0 copy-done.7
  9.5 0.0 copy-done.8
  9.5 0.0 copy-done.9
  9.5 4.0 %shard_map.155 = (f32[400,128]{1,0:T(8,128)S(1)}, f32[1,128]{1,0:T(1,128)S(1)}, f32[2,400,256]{2,1,0:T(8,128)S(1)}, f32[400,512]{1,0:T(8,128)S(1)}, f32[400,256]{1,0:T(8,128)S(1)}, /*index=5*/f32[400,512]{1,0:T(8,128)S(1)}) custom-call(f32[400,128]{1,0:T(8,128)S(1)} %bitcast.24, f32[400,128]{1,0:T(8,128)S(1)} %bitcast.26, f32[1,128]{1,0:T(1,128)S(1)} %copy-done.8, ...), custom_call_target="tpu_custom_call" | custom-call | flops 4000000000 | bytes 4316168 | tf_op jit(solution)/shard_map/pallas_call | solution.py:208
  13.6 0.0 collective-permute-done.moved
  13.6 1.8 %shard_map.156 = (f32[400,512]{1,0:T(8,128)S(1)}, f32[1,512]{1,0:T(1,128)S(1)}, f32[256,512]{1,0:T(8,128)S(1)}, f32[400,512]{1,0:T(8,128)S(1)}, f32[400,512]{1,0:T(8,128)S(1)}, /*index=5*/f32[800,128]{1,0:T(8,128)S(1)}) custom-call(f32[408,128]{1,0:T(8,128)S(1)} %collective-permute-done.moved, f32[400,512]{1,0:T(8,128)S(1)} %get-tuple-element.28.right, ...), custom_call_target="tpu_custom_call" | custom-call | flops 2000000000 | bytes 6477832 | tf_op jit(solution)/shard_map/pallas_call | solution.py:208
  15.4 2.0 %collective-permute-start.1 = (f32[800,128]{1,0:T(8,128)S(1)}, f32[800,128]{1,0:T(8,128)S(1)}, u32[]{:S(2)}, u32[]{:S(2)}) collective-permute-start(f32[800,128]{1,0:T(8,128)S(1)} %get-tuple-element.41), channel_id=1, source_target_pairs={{0,4},{4,0},{1,5},{5,1},{2,6},{6,2},{3,7},{7,3},{8,12},{12,8},{9,1... | collective-permute-start | bytes 1228808 | tf_op jit(solution)/shard_map/ppermute | solution.py:228
  17.4 2.2 %shard_map.157 = (f32[400,128]{1,0:T(8,128)}, f32[1,128]{1,0:T(1,128)}, f32[400,128]{1,0:T(8,128)}, f32[1,128]{1,0:T(1,128)}, f32[800,128]{1,0:T(8,128)S(1)}) custom-call(f32[408,128]{1,0:T(8,128)S(1)} %collective-permute-done.moved, f32[400,128]{1,0:T(8,128)S(1)} %get-tuple-element.25.target, f32[1,128]{1,0:T(1,128)S(1)} %get-tuple-element.26.target_acc, ...), custom_call_target="tpu_custom_call" | custom-call | flops 2000000000 | bytes 5871104 | tf_op jit(solution)/shard_map/pallas_call | solution.py:208
  19.5 0.0 collective-permute-done.1
  19.6 23.3 %all_to_all.15 = f32[32,1,3200]{2,1,0:T(1,128)S(1)} all-to-all(f32[32,1,3200]{2,1,0:T(1,128)S(1)} %bitcast.30), channel_id=1, replica_groups={{0,8,16,24,32,40,48,56,128,136,144,152,160,168,176,184,256,264,272,280,..., dimensions={0} | all-to-all | bytes 819200 | tf_op jit(solution)/shard_map/all_to_all | solution.py:220
  42.9 0.2 reduce_sum.18
  43.2 0.1 broadcast_in_dim.23
  43.2 16.9 %all_to_all.16 = f32[8,1,3200]{2,1,0:T(1,128)S(1)} all-to-all(f32[8,1,3200]{2,1,0:T(1,128)S(1)} %broadcast_in_dim.23), channel_id=1, replica_groups={{0,1,2,3,64,65,66,67},{8,9,10,11,72,73,74,75},{16,17,18,19,80,81,82,83}..., dimensions={0} | all-to-all | bytes 204800 | tf_op jit(solution)/shard_map/all_to_all | solution.py:220
  60.2 0.1 reduce_sum.19
  60.3 0.2 broadcast_in_dim.24
  60.5 15.7 %all_to_all.17 = f32[32,1,3200]{2,1,0:T(1,128)S(1)} all-to-all(f32[32,1,3200]{2,1,0:T(1,128)S(1)} %broadcast_in_dim.24), channel_id=1, replica_groups={{0,8,16,24,32,40,48,56,128,136,144,152,160,168,176,184,256,264,272,280,..., dimensions={0} | all-to-all | bytes 819200 | tf_op jit(solution)/shard_map/all_to_all | solution.py:220
  76.2 0.0 copy-start.1
  76.2 7.3 %all_gather.3.sums = f32[1600,128]{1,0:T(8,128)S(1)} all-gather(f32[800,128]{1,0:T(8,128)S(1)} %bitcast.31), channel_id=1, replica_groups=mesh['x'=4,'h'=2,'y'=8,'c'=2,'l'=4] {'c'}, dimensions={0}, use_global_device_ids=true | all-gather | bytes 1228800 | tf_op jit(solution)/shard_map/all_gather | solution.py:268
  83.5 0.0 copy-done.1
  83.5 1.2 %shard_map.158 = (f32[400,512]{1,0:T(8,128)}, f32[1,512]{1,0:T(1,128)}) custom-call(f32[1600,128]{1,0:T(8,128)S(1)} %all_gather.3.sums, f32[400,512]{1,0:T(8,128)S(1)} %bitcast.21, f32[1,512]{1,0:T(1,128)S(1)} %bitcast.22), custom_call_target="tpu_custom_call" | custom-call | bytes 2461696 | tf_op jit(solution)/shard_map/pallas_call | solution.py:208
  (1 shorter events, 0.0 us)
Async XLA Ops:
  0.6 8.8 %copy-start = (f32[512,400]{0,1:T(8,128)S(1)}, f32[512,400]{0,1:T(8,128)}, u32[]{:S(2)}) copy-start(f32[512,400]{0,1:T(8,128)} %param.15) | copy-start | bytes 2457604
  0.6 8.8 %copy-start.2 = (f32[1,128,400]{1,2,0:T(8,128)S(1)}, f32[1,128,400]{1,2,0:T(8,128)}, u32[]{:S(2)}) copy-start(f32[1,128,400]{1,2,0:T(8,128)} %param.11) | copy-start | bytes 614404
  0.7 8.8 %copy-start.3 = (f32[1,128,400]{1,2,0:T(8,128)S(1)}, f32[1,128,400]{1,2,0:T(8,128)}, u32[]{:S(2)}) copy-start(f32[1,128,400]{1,2,0:T(8,128)} %param.13) | copy-start | bytes 614404
  0.7 8.8 %copy-start.4 = (s32[2,1,1,512]{3,2,1,0:T(1,128)S(1)}, s32[2,1,1,512]{3,2,1,0:T(1,128)}, u32[]{:S(2)}) copy-start(s32[2,1,1,512]{3,2,1,0:T(1,128)} %kid.5) | copy-start | bytes 12292
  0.7 8.8 %copy-start.5 = (s32[2,1,1,512]{3,2,1,0:T(1,128)S(1)}, s32[2,1,1,512]{3,2,1,0:T(1,128)}, u32[]{:S(2)}) copy-start(s32[2,1,1,512]{3,2,1,0:T(1,128)} %sid.5) | copy-start | bytes 12292
  0.7 8.8 %copy-start.6 = (s32[2,1,1,512]{3,2,1,0:T(1,128)S(1)}, s32[2,1,1,512]{3,2,1,0:T(1,128)}, u32[]{:S(2)}) copy-start(s32[2,1,1,512]{3,2,1,0:T(1,128)} %tid.3) | copy-start | bytes 12292
  0.7 8.8 %copy-start.7 = (s32[2,1,1,1,256]{4,3,2,1,0:T(1,128)S(1)}, s32[2,1,1,1,256]{4,3,2,1,0:T(1,128)}, u32[]{:S(2)}) copy-start(s32[2,1,1,1,256]{4,3,2,1,0:T(1,128)} %nid.3) | copy-start | bytes 6148
  0.7 8.8 %copy-start.8 = (f32[1,128]{1,0:T(1,128)S(1)}, f32[1,128]{1,0:T(1,128)}, u32[]{:S(2)}) copy-start(f32[1,128]{1,0:T(1,128)} %target_acc.1) | copy-start | bytes 1540
  0.7 8.8 %copy-start.9 = (s32[2,1,1]{0,2,1:T(1,128)S(1)}, s32[2,1,1]{0,2,1:T(1,128)}, u32[]{:S(2)}) copy-start(s32[2,1,1]{0,2,1:T(1,128)} %param.20) | copy-start | bytes 28
  5.7 7.9 %collective-permute-start = (f32[408,128]{1,0:T(8,128)}, f32[408,128]{1,0:T(8,128)S(1)}, u32[]{:S(2)}, u32[]{:S(2)}) collective-permute-start(f32[408,128]{1,0:T(8,128)} %shard_map.154), channel_id=1, source_target_pairs={{0,4},{4,8},{8,12},{12,16},{16,20},{20,24},{24,28},{28,32},{32,36}... | collective-permute-start | bytes 626696 | tf_op jit(solution)/shard_map/ppermute | solution.py:248
  15.4 4.2 %collective-permute-start.1 = (f32[800,128]{1,0:T(8,128)S(1)}, f32[800,128]{1,0:T(8,128)S(1)}, u32[]{:S(2)}, u32[]{:S(2)}) collective-permute-start(f32[800,128]{1,0:T(8,128)S(1)} %get-tuple-element.41), channel_id=1, source_target_pairs={{0,4},{4,0},{1,5},{5,1},{2,6},{6,2},{3,7},{7,3},{8,12},{12,8},{9,1... | collective-permute-start | bytes 1228808 | tf_op jit(solution)/shard_map/ppermute | solution.py:228
  76.2 7.3 %copy-start.1 = (f32[512]{0:T(512)S(1)}, f32[512]{0:T(512)}, u32[]{:S(2)}) copy-start(f32[512]{0:T(512)} %param.16) | copy-start | bytes 6148

commit v3 on v2

--- a/solution.py
+++ b/solution.py
@@ -87,37 +87,30 @@
     return scatter(pull * query, target_hot) + scatter(to_samples, sample_hot)
 
 
-def bucket(source, target, scale, sid, tid, nid, cnt):
-    left = gather(source, one_hot(sid, LANES))
-    right = gather(target, one_hot(tid, LANES))
-    sampled = gather(target, one_hot(nid, LANES))
+def bucket(left, right, sampled, scale, cnt):
     query = left * scale
     pull, push = scores(query, right, sampled, cnt)
     grad_query = pull * right + product3(split(sampled), split(push))
-    return left, query, pull, push, grad_query
-
-
-def first_source(
-    kid_in, relation_in, sid_in, source_in, tid_in, target_in, nid_in, cnt_in, source_acc_in, moved,
-    kid, relation, sid, source, tid, target, nid, cnt, source_acc, arrived,
-):
-    wanted = (
-        (kid_in, kid), (relation_in, relation), (sid_in, sid), (source_in, source), (tid_in, tid),
-        (target_in, target), (nid_in, nid), (cnt_in, cnt), (source_acc_in, source_acc),
-    )
-    copies = [pltpu.make_async_copy(a, b, arrived.at[i]) for i, (a, b) in enumerate(wanted)]
+    return query, pull, push, grad_query
+
+
+def first_source(*refs):
+    count = (len(refs) - 2) // 2
+    moved, arrived = refs[count], refs[-1]
+    fetched = refs[count + 1 : -1]
+    sid, source, tid, target, nid, kid, relation, cnt, source_acc = fetched[:9]
+    copies = [pltpu.make_async_copy(refs[i], fetched[i], arrived.at[i]) for i in range(count)]
     for copy in copies:
         copy.start()
-    copies[0].wait()
-    kind_hot = one_hot(kid[0, 0], relation.shape[1])
-    copies[1].wait()
-    scale = gather(relation[...], kind_hot)
-    for copy in copies[2:]:
+    for copy in copies:
         copy.wait()
-    grad_query = bucket(
-        source[...], target[...], scale, sid[0, 0], tid[0, 0], nid[0, 0, 0], cnt[0, :, 0:1]
-    )[-1]
-    grads = scatter(grad_query * scale, one_hot(sid[0, 0], LANES))
+    source_hot = one_hot(sid[0, 0], LANES)
+    left = gather(source[...], source_hot)
+    right = gather(target[...], one_hot(tid[0, 0], LANES))
+    sampled = gather(target[...], one_hot(nid[0, 0, 0], LANES))
+    scale = gather(relation[...], one_hot(kid[0, 0], relation.shape[1]))
+    grad_query = bucket(left, right, sampled, scale, cnt[0, :, 0:1])[-1]
+    grads = scatter(grad_query * scale, source_hot)
     rows, acc = adagrad(source[...], source_acc[...], grads, learning_rate)
     width = source.shape[0]
     moved[0:width, :] = rows
@@ -129,11 +122,13 @@
     target_out, target_acc_out, total, right_out, sampled_out, scale_out,
 ):
     kind_hot = one_hot(kid[0, 0], relation.shape[1])
-    left, query, pull, push, grad_query = bucket(
-        source[...], target[...], gather(relation[...], kind_hot), sid[0, 0], tid[0, 0], nid[0, 0, 0],
+    target_hot, sample_hot = one_hot(tid[0, 0], LANES), one_hot(nid[0, 0, 0], LANES)
+    left = gather(source[...], one_hot(sid[0, 0], LANES))
+    query, pull, push, grad_query = bucket(
+        left, gather(target[...], target_hot), gather(target[...], sample_hot), gather(relation[...], kind_hot),
         cnt[0, :, 0:1],
     )
-    grads = target_grads(query, pull, push, one_hot(tid[0, 0], LANES), one_hot(nid[0, 0, 0], LANES))
+    grads = target_grads(query, pull, push, target_hot, sample_hot)
     rows, acc = adagrad(target[...], target_acc[...], grads, learning_rate)
     target_out[...] = rows
     target_acc_out[...] = acc
@@ -200,18 +195,23 @@
 
 
 def call(kernel, shapes, *operands, flops=0, fetch=False):
-    scratch = []
+    outs = [jax.ShapeDtypeStruct(s, F32) for s in shapes]
+    scratch, spec = [], VM
     if fetch:
-        scratch = [pltpu.VMEM(o.shape, o.dtype) for o in operands]
-        scratch.append(pltpu.SemaphoreType.DMA((len(operands),)))
-    moved = sum(4 * int(np.prod(s)) for s in shapes) + sum(4 * o.size for o in operands)
+        outs += [pltpu.VMEM(o.shape, o.dtype) for o in operands]
+        outs[0] = pltpu.VMEM(shapes[0], F32)
+        scratch = [pltpu.SemaphoreType.DMA((len(operands),))]
+        spec = pl.BlockSpec(memory_space=pltpu.HBM)
+    moved = sum(4 * int(np.prod(o.shape)) for o in outs) + sum(4 * o.size for o in operands)
+    if fetch:
+        operands = [pltpu.with_memory_space_constraint(o, pltpu.HBM) for o in operands]
     return pl.pallas_call(
         kernel,
-        out_shape=[jax.ShapeDtypeStruct(s, F32) for s in shapes],
-        in_specs=[pl.BlockSpec(memory_space=pltpu.HBM) if fetch else VM] * len(operands),
-        out_specs=[VM] * len(shapes),
+        out_shape=outs,
+        in_specs=[spec] * len(operands),
+        out_specs=[VM] * len(outs),
         scratch_shapes=scratch,
-        compiler_params=pltpu.CompilerParams(vmem_limit_bytes=(60 if fetch else 40) * 2**20),
+        compiler_params=pltpu.CompilerParams(vmem_limit_bytes=40 * 2**20),
         cost_estimate=pl.CostEstimate(flops=flops, bytes_accessed=moved, transcendentals=0),
     )(*operands)
 
@@ -240,9 +240,10 @@
     edges, pairs = (width, slots), (negatives, slots)
     blocks = (width * kinds // 2 // LANES, LANES)
     work = 10**9
-    (moved,) = call(
+    moved, sid, source, tid, target, nid, kid, relation, cnt, _, target_state, relation_state = call(
         first_source, [(width + 8, LANES)],
-        kid, relation, sid, source, tid, target, nid, cnt, source_state, flops=2 * work, fetch=True,
+        sid, source, tid, target, nid, kid, relation, cnt, source_state, target_state, relation_state[None],
+        flops=2 * work, fetch=True,
     )
     count = lax.axis_size(BLK)
     moved = lax.ppermute(moved, BLK, [(i, (i + 1) % count) for i in range(count)])
@@ -267,7 +268,7 @@
     halves = exchange(spread(block, in_plane), planes).reshape(blocks)
     sums = lax.all_gather(halves, "c", tiled=True)
     relation, relation_acc = call(
-        last_update, [(width, kinds), (1, kinds)], sums, relation, relation_state[None]
+        last_update, [(width, kinds), (1, kinds)], sums, relation, relation_state
     )
     return (source.T[None], source_acc, target.T[None], target_acc, relation.T, relation_acc[0])
 

time: 85 us -> 83.7 us (0.985)
  Pallas kernels: 14.1 us -> 12.9 us
    pallas_call x5, Pallas kernels: 14.1 us -> 12.9 us  [call(): pl.pallas_call(kernel, out_shape=outs, in_specs=[spec] * len(operands), o...]
where the time goes in v3:
time: 83.7 us; the launch traced here: 83.4 us
  blocking collectives  63.2 us (76%)
  Pallas kernels  12.9 us (15%)
  starting transfers between devices  5.99 us (7%)
    all_to_all x3, blocking collectives, exchange(): lax.all_to_all(blocks, AXES, 0, 0, axis_index_groups=groups, tiled=True)  56 us
    pallas_call x5, Pallas kernels, call(): pl.pallas_call(kernel, out_shape=outs, in_specs=[spec] * len(operands), o...  12.9 us
    all_gather x1, blocking collectives, on_device(): sums = lax.all_gather(halves, 'c', tiled=True)  7.21 us
    ppermute x1, starting transfers between devices, on_device(): lax.ppermute(moved, BLK, [(i, (i + 1) % count) for i in range(count)])  3.76 us
    ppermute x1, starting transfers between devices, swap_cores(): return lax.ppermute(value, 'c', [(0, 1), (1, 0)])  2.22 us
  transfers between devices with their start and end apart: 2, of which 0 were waited for; matrix products, arithmetic and copies ran while one was open for 0% of the time, Pallas kernels for 7%

profile of v3, /device:TPU:9, one launch (start us, length us, event | category | flops | bytes accessed | tf_op | source)
XLA Modules:
  0.0 83.4 jit_solution(2457015986558551944)
XLA Ops:
  0.6 4.1 %shard_map.154 = (f32[408,128]{1,0:T(8,128)S(1)}, s32[2,1,1,512]{3,2,1,0:T(1,128)S(1)}, f32[400,128]{1,0:T(8,128)S(1)}, s32[2,1,1,512]{3,2,1,0:T(1,128)S(1)}, f3...) custom-call(s32[2,1,1,512]{3,2,1,0:T(1,128)} %refs_0_.1, ...), custom_call_target="tpu_custom_call" | custom-call | flops 2000000000 | bytes 2701328 | tf_op jit(solution)/shard_map/pallas_call | solution.py:208
  4.7 3.8 %collective-permute-start = (f32[408,128]{1,0:T(8,128)S(1)}, f32[408,128]{1,0:T(8,128)S(1)}, u32[]{:S(2)}, u32[]{:S(2)}) collective-permute-start(f32[408,128]{1,0:T(8,128)S(1)} %get-tuple-element.36), channel_id=1, source_target_pairs={{0,4},{4,8},{8,12},{12,16},{16,20},{20,24},{24,28},{28,32},{32,36}... | collective-permute-start | bytes 626696 | tf_op jit(solution)/shard_map/ppermute | solution.py:249
  8.5 3.7 %shard_map.155 = (f32[400,128]{1,0:T(8,128)S(1)}, f32[1,128]{1,0:T(1,128)S(1)}, f32[2,400,256]{2,1,0:T(8,128)S(1)}, f32[400,512]{1,0:T(8,128)S(1)}, f32[400,256]{1,0:T(8,128)S(1)}, /*index=5*/f32[400,512]{1,0:T(8,128)S(1)}) custom-call(f32[400,128]{1,0:T(8,128)S(1)} %get-tuple-element.37.source, f32[400,128]{1,0:T(8,128)S(1)} %get-tuple-element.38.target, ...), custom_call_target="tpu_custom_call" | custom-call | flops 4000000000 | bytes 4316168 | tf_op jit(solution)/shard_map/pallas_call | solution.py:208
  12.2 0.0 collective-permute-done.moved
  12.2 1.8 %shard_map.156 = (f32[400,512]{1,0:T(8,128)S(1)}, f32[1,512]{1,0:T(1,128)S(1)}, f32[256,512]{1,0:T(8,128)S(1)}, f32[400,512]{1,0:T(8,128)S(1)}, f32[400,512]{1,0:T(8,128)S(1)}, /*index=5*/f32[800,128]{1,0:T(8,128)S(1)}) custom-call(f32[408,128]{1,0:T(8,128)S(1)} %collective-permute-done.moved, f32[400,512]{1,0:T(8,128)S(1)} %get-tuple-element.49.right, ...), custom_call_target="tpu_custom_call" | custom-call | flops 2000000000 | bytes 6477832 | tf_op jit(solution)/shard_map/pallas_call | solution.py:208
  14.0 2.2 %collective-permute-start.1 = (f32[800,128]{1,0:T(8,128)S(1)}, f32[800,128]{1,0:T(8,128)S(1)}, u32[]{:S(2)}, u32[]{:S(2)}) collective-permute-start(f32[800,128]{1,0:T(8,128)S(1)} %get-tuple-element.62), channel_id=1, source_target_pairs={{0,4},{4,0},{1,5},{5,1},{2,6},{6,2},{3,7},{7,3},{8,12},{12,8},{9,1... | collective-permute-start | bytes 1228808 | tf_op jit(solution)/shard_map/ppermute | solution.py:228
  16.2 2.2 %shard_map.157 = (f32[400,128]{1,0:T(8,128)}, f32[1,128]{1,0:T(1,128)}, f32[400,128]{1,0:T(8,128)}, f32[1,128]{1,0:T(1,128)}, f32[800,128]{1,0:T(8,128)S(1)}) custom-call(f32[408,128]{1,0:T(8,128)S(1)} %collective-permute-done.moved, f32[400,128]{1,0:T(8,128)S(1)} %get-tuple-element.46.target, f32[1,128]{1,0:T(1,128)S(1)} %get-tuple-element.47.target_acc, ...), custom_call_target="tpu_custom_call" | custom-call | flops 2000000000 | bytes 5871104 | tf_op jit(solution)/shard_map/pallas_call | solution.py:208
  18.4 0.0 collective-permute-done.1
  18.4 23.3 %all_to_all.15 = f32[32,1,3200]{2,1,0:T(1,128)S(1)} all-to-all(f32[32,1,3200]{2,1,0:T(1,128)S(1)} %bitcast.19), channel_id=1, replica_groups={{0,8,16,24,32,40,48,56,128,136,144,152,160,168,176,184,256,264,272,280,..., dimensions={0} | all-to-all | bytes 819200 | tf_op jit(solution)/shard_map/all_to_all | solution.py:220
  41.8 0.2 reduce_sum.18
  42.0 0.1 broadcast_in_dim.24
  42.1 17.0 %all_to_all.16 = f32[8,1,3200]{2,1,0:T(1,128)S(1)} all-to-all(f32[8,1,3200]{2,1,0:T(1,128)S(1)} %broadcast_in_dim.24), channel_id=1, replica_groups={{0,1,2,3,64,65,66,67},{8,9,10,11,72,73,74,75},{16,17,18,19,80,81,82,83}..., dimensions={0} | all-to-all | bytes 204800 | tf_op jit(solution)/shard_map/all_to_all | solution.py:220
  59.0 0.1 reduce_sum.19
  59.1 0.2 broadcast_in_dim.25
  59.4 15.7 %all_to_all.17 = f32[32,1,3200]{2,1,0:T(1,128)S(1)} all-to-all(f32[32,1,3200]{2,1,0:T(1,128)S(1)} %broadcast_in_dim.25), channel_id=1, replica_groups={{0,8,16,24,32,40,48,56,128,136,144,152,160,168,176,184,256,264,272,280,..., dimensions={0} | all-to-all | bytes 819200 | tf_op jit(solution)/shard_map/all_to_all | solution.py:220
  75.0 7.2 %all_gather.3.sums = f32[1600,128]{1,0:T(8,128)S(1)} all-gather(f32[800,128]{1,0:T(8,128)S(1)} %bitcast.20), channel_id=1, replica_groups=mesh['x'=4,'h'=2,'y'=8,'c'=2,'l'=4] {'c'}, dimensions={0}, use_global_device_ids=true | all-gather | bytes 1228800 | tf_op jit(solution)/shard_map/all_gather | solution.py:269
  82.2 1.2 %shard_map.158 = (f32[400,512]{1,0:T(8,128)}, f32[1,512]{1,0:T(1,128)}) custom-call(f32[1600,128]{1,0:T(8,128)S(1)} %all_gather.3.sums, f32[400,512]{1,0:T(8,128)S(1)} %get-tuple-element.40.relation, f32[1,512]{1,0:T(1,128)S(1)} %get-tuple-element.63.relation_acc), custom_call_target="tpu_custom_call" | custom-call | bytes 2461696 | tf_op jit(solution)/shard_map/pallas_call | solution.py:208
  (1 shorter events, 0.0 us)
Async XLA Ops:
  4.7 7.5 %collective-permute-start = (f32[408,128]{1,0:T(8,128)S(1)}, f32[408,128]{1,0:T(8,128)S(1)}, u32[]{:S(2)}, u32[]{:S(2)}) collective-permute-start(f32[408,128]{1,0:T(8,128)S(1)} %get-tuple-element.36), channel_id=1, source_target_pairs={{0,4},{4,8},{8,12},{12,16},{16,20},{20,24},{24,28},{28,32},{32,36}... | collective-permute-start | bytes 626696 | tf_op jit(solution)/shard_map/ppermute | solution.py:249
  14.0 4.4 %collective-permute-start.1 = (f32[800,128]{1,0:T(8,128)S(1)}, f32[800,128]{1,0:T(8,128)S(1)}, u32[]{:S(2)}, u32[]{:S(2)}) collective-permute-start(f32[800,128]{1,0:T(8,128)S(1)} %get-tuple-element.62), channel_id=1, source_target_pairs={{0,4},{4,0},{1,5},{5,1},{2,6},{6,2},{3,7},{7,3},{8,12},{12,8},{9,1... | collective-permute-start | bytes 1228808 | tf_op jit(solution)/shard_map/ppermute | solution.py:228

commit v4 on v3

--- a/solution.py
+++ b/solution.py
@@ -1,3 +1,5 @@
+import functools
+
 import jax
 import jax.numpy as jnp
 import numpy as np
@@ -46,7 +48,8 @@
 def product3(left, right, dims=((1,), (0,))):
     lh, ll = left
     rh, rl = right
-    return product(lh, rh, dims) + product(lh, rl, dims) + product(ll, rh, dims)
+    (a,), (b,) = dims
+    return product(jnp.concatenate([lh, lh, ll], a), jnp.concatenate([rh, rl, rh], b), dims)
 
 
 def one_hot(ids, count):
@@ -62,9 +65,9 @@
 
 
 def scatter(values, hot):
-    high, low = split(values)
-    across = ((1,), (1,))
-    return product(high, hot, across) + product(low, hot, across)
+    count = values.shape[0]
+    both = product(jnp.concatenate(split(values), 0), hot, ((1,), (1,)))
+    return both[:count] + both[count:]
 
 
 def adagrad(weights, accum, grads, rate):
@@ -147,42 +150,46 @@
         out[block * width : (block + 1) * width, :] = sums[:, block * LANES : (block + 1) * LANES]
 
 
-def second_edges(
-    moved, right, sampled, scale, sid, kid, cnt, total,
-    query_out, pull_out, push_out, grad_out, typed_out, sent,
-):
+def second_edges(moved, right, sampled, scale, sid, kid, cnt, total, sent, kept):
     width = right.shape[0]
     left = gather(moved[0:width, :], one_hot(sid[1, 0], LANES))
-    query = left * scale[...]
-    pull, push = scores(query, right[...], sampled[...], cnt[0, :, 1:2])
-    grad_query = pull * right[...] + product3(split(sampled[...]), split(push))
-    typed = grad_query * left
-    other = 1 - lax.axis_index("c")
+    grad_query = bucket(left, right[...], sampled[...], scale[...], cnt[0, :, 1:2])[-1]
+    typed = jnp.concatenate(split(grad_query * left), 0)
+    me = lax.axis_index("c")
     half = total.shape[2]
-    put_blocks(sent, total[other] + scatter(typed, one_hot(kid[1, 0] - other * half, half)))
-    query_out[...] = query
-    pull_out[...] = pull
-    push_out[...] = push
-    grad_out[...] = grad_query
-    typed_out[...] = typed
+    for blocks, mine in ((sent, 1 - me), (kept, me)):
+        both = product(typed, one_hot(kid[1, 0] - mine * half, half), ((1,), (1,)))
+        put_blocks(blocks, total[mine] + both[:width] + both[width:])
 
 
 def second_rest(
-    moved, target, target_acc, scale, sid, tid, kid, nid, query, pull, push, grad_query, typed, total,
-    source_out, source_acc_out, target_out, target_acc_out, kept,
+    moved, target, target_acc, right, sampled, scale, sid, tid, nid, cnt,
+    source_out, source_acc_out, target_out, target_acc_out,
 ):
     width = target.shape[0]
-    me = lax.axis_index("c")
-    half = total.shape[2]
-    put_blocks(kept, total[me] + scatter(typed[...], one_hot(kid[1, 0] - me * half, half)))
-    grads = target_grads(
-        query[...], pull[...], push[...], one_hot(tid[1, 0], LANES), one_hot(nid[1, 0, 0], LANES)
-    )
+    source_hot = one_hot(sid[1, 0], LANES)
+    left = gather(moved[0:width, :], source_hot)
+    query, pull, push, grad_query = bucket(left, right[...], sampled[...], scale[...], cnt[0, :, 1:2])
+    grads = target_grads(query, pull, push, one_hot(tid[1, 0], LANES), one_hot(nid[1, 0, 0], LANES))
     target_out[...], target_acc_out[...] = adagrad(target[...], target_acc[...], grads, learning_rate)
-    grads = scatter(grad_query[...] * scale[...], one_hot(sid[1, 0], LANES))
+    grads = scatter(grad_query * scale[...], source_hot)
     source_out[...], source_acc_out[...] = adagrad(
         moved[0:width, :], moved[width : width + 1, :], grads, learning_rate
     )
+
+
+def add_received(both, kept, out):
+    out[...] = kept[...] + both[1 - lax.axis_index("c")]
+
+
+def fold(parts, out, *, copies):
+    block = out.shape[0] // copies
+    count = parts.shape[0] // block
+    total = parts[0:block, :]
+    for i in range(1, count):
+        total += parts[i * block : (i + 1) * block, :]
+    for i in range(copies):
+        out[i * block : (i + 1) * block, :] = total
 
 
 def last_update(sums, relation, relation_acc, relation_out, relation_acc_out):
@@ -194,9 +201,11 @@
         )
 
 
-def call(kernel, shapes, *operands, flops=0, fetch=False):
+def call(kernel, shapes, *operands, flops=0, fetch=False, pinned=False):
     outs = [jax.ShapeDtypeStruct(s, F32) for s in shapes]
     scratch, spec = [], VM
+    if pinned:
+        outs = [pltpu.VMEM(s, F32) for s in shapes]
     if fetch:
         outs += [pltpu.VMEM(o.shape, o.dtype) for o in operands]
         outs[0] = pltpu.VMEM(shapes[0], F32)
@@ -211,9 +220,13 @@
         in_specs=[spec] * len(operands),
         out_specs=[VM] * len(outs),
         scratch_shapes=scratch,
-        compiler_params=pltpu.CompilerParams(vmem_limit_bytes=40 * 2**20),
+        compiler_params=pltpu.CompilerParams(vmem_limit_bytes=16 * 2**20),
         cost_estimate=pl.CostEstimate(flops=flops, bytes_accessed=moved, transcendentals=0),
     )(*operands)
+
+
+def in_vmem(value):
+    return pltpu.with_memory_space_constraint(value, pltpu.VMEM)
 
 
 def exchange(blocks, groups):
@@ -237,7 +250,7 @@
     width, kinds = relation.shape
     slots, negatives = sid.shape[-1], nid.shape[-1]
     table, row = (width, LANES), (1, LANES)
-    edges, pairs = (width, slots), (negatives, slots)
+    edges = (width, slots)
     blocks = (width * kinds // 2 // LANES, LANES)
     work = 10**9
     moved, sid, source, tid, target, nid, kid, relation, cnt, _, target_state, relation_state = call(
@@ -251,21 +264,24 @@
         first_rest, [table, row, (2, width, kinds // 2), edges, (width, negatives), edges],
         source, target, target_state, relation, sid, tid, kid, nid, cnt, flops=4 * work,
     )
-    query, pull, push, grad_query, typed, sent = call(
-        second_edges, [edges, (1, slots), pairs, edges, edges, blocks],
-        moved, right, sampled, scale, sid, kid, cnt, total, flops=2 * work,
-    )
-    received = swap_cores(sent)
-    source, source_acc, target, target_acc, kept = call(
-        second_rest, [table, row, table, row, blocks],
-        moved, target, target_acc, scale, sid, tid, kid, nid, query, pull, push, grad_query, typed, total,
-        flops=2 * work,
+    sent, kept = call(
+        second_edges, [blocks, blocks], moved, right, sampled, scale, sid, kid, cnt, total, flops=2 * work
+    )
+    both = lax.all_gather(sent, "c")
+    parts = call(add_received, [blocks], both, kept, pinned=True)[0]
+    source, source_acc, target, target_acc = call(
+        second_rest, [table, row, table, row],
+        moved, target, target_acc, right, sampled, scale, sid, tid, nid, cnt, flops=4 * work,
     )
     planes, lines = plane_groups(), line_groups()
     in_plane, in_line = len(planes[0]), len(lines[0])
-    block = jnp.sum(exchange((kept + received).reshape(in_plane, 1, -1), planes), 0)
-    block = jnp.sum(exchange(spread(block, in_line), lines), 0)
-    halves = exchange(spread(block, in_plane), planes).reshape(blocks)
+    share = blocks[0] // in_plane
+    parts = exchange(parts.reshape(in_plane, 1, -1), planes).reshape(blocks)
+    (block,) = call(functools.partial(fold, copies=in_line), [(share * in_line, LANES)], in_vmem(parts))
+    block, source_acc = lax.optimization_barrier((block, source_acc))
+    parts = exchange(block.reshape(in_line, 1, -1), lines).reshape(share * in_line, LANES)
+    (block,) = call(functools.partial(fold, copies=in_plane), [blocks], in_vmem(parts))
+    halves = exchange(block.reshape(in_plane, 1, -1), planes).reshape(blocks)
     sums = lax.all_gather(halves, "c", tiled=True)
     relation, relation_acc = call(
         last_update, [(width, kinds), (1, kinds)], sums, relation, relation_state

time: 83.7 us -> 82.1 us (0.981)
  blocking collectives: 63.2 us -> 42.8 us
  starting transfers between devices: 5.99 us -> 16.6 us
  waiting for transfers between devices: 0.01 us -> 6.35 us
  Pallas kernels: 12.9 us -> 14.4 us
    all_to_all x3 -> x2, blocking collectives: 56 us -> 33 us  [exchange(): lax.all_to_all(blocks, AXES, 0, 0, axis_index_groups=groups, tiled=True)]
    all_to_all x0 -> x1, starting transfers between devices: none -> 12.9 us  [exchange(): lax.all_to_all(blocks, AXES, 0, 0, axis_index_groups=groups, tiled=True)]
    all_to_all x0 -> x1, waiting for transfers between devices: none -> 6.35 us  [exchange(): lax.all_to_all(blocks, AXES, 0, 0, axis_index_groups=groups, tiled=True)]
    all_gather x0 -> x1, blocking collectives: none -> 2.39 us  [on_device(): both = lax.all_gather(sent, 'c')]
    ppermute x1 -> x0, starting transfers between devices: 2.22 us -> none  [swap_cores(): return lax.ppermute(value, 'c', [(0, 1), (1, 0)])]
    pallas_call x5 -> x8, Pallas kernels: 12.9 us -> 14.4 us  [call(): pl.pallas_call(kernel, out_shape=outs, in_specs=[spec] * len(operands), o...]
    unnamed x0 -> x4, local copies, waits for them, and re-layouts: none -> 0.93 us
  transfers between devices with their start and end apart: 2 -> 2, of which waited for: 0 -> 1; matrix products, arithmetic and copies ran while one was open for 0% -> 0% of each run, Pallas kernels for 7% -> 8%
where the time goes in v4:
time: 82.1 us; the launch traced here: 81.8 us
  blocking collectives  42.8 us (52%)
  starting transfers between devices  16.6 us (20%)
  Pallas kernels  14.4 us (18%)
  waiting for transfers between devices  6.35 us (8%)
  local copies, waits for them, and re-layouts  0.93 us (1%)
    all_to_all x2, blocking collectives, exchange(): lax.all_to_all(blocks, AXES, 0, 0, axis_index_groups=groups, tiled=True)  33 us
    pallas_call x8, Pallas kernels, call(): pl.pallas_call(kernel, out_shape=outs, in_specs=[spec] * len(operands), o...  14.4 us
    all_to_all x1, starting transfers between devices, exchange(): lax.all_to_all(blocks, AXES, 0, 0, axis_index_groups=groups, tiled=True)  12.9 us
    all_gather x1, blocking collectives, on_device(): sums = lax.all_gather(halves, 'c', tiled=True)  7.34 us
    all_to_all x1, waiting for transfers between devices, exchange(): lax.all_to_all(blocks, AXES, 0, 0, axis_index_groups=groups, tiled=True)  6.35 us
    ppermute x1, starting transfers between devices, on_device(): lax.ppermute(moved, BLK, [(i, (i + 1) % count) for i in range(count)])  3.77 us
    all_gather x1, blocking collectives, on_device(): both = lax.all_gather(sent, 'c')  2.39 us
  transfers between devices with their start and end apart: 2, of which 1 were waited for; matrix products, arithmetic and copies ran while one was open for 0% of the time, Pallas kernels for 8%

profile of v4, /device:TPU:9, one launch (start us, length us, event | category | flops | bytes accessed | tf_op | source)
XLA Modules:
  0.0 81.8 jit_solution(5910145668527249253)
XLA Ops:
  0.6 3.7 %shard_map.154 = (f32[408,128]{1,0:T(8,128)S(1)}, s32[2,1,1,512]{3,2,1,0:T(1,128)S(1)}, f32[400,128]{1,0:T(8,128)S(1)}, s32[2,1,1,512]{3,2,1,0:T(1,128)S(1)}, f3...) custom-call(s32[2,1,1,512]{3,2,1,0:T(1,128)} %refs_0_.1, ...), custom_call_target="tpu_custom_call" | custom-call | flops 2000000000 | bytes 2701328 | tf_op jit(solution)/shard_map/pallas_call | solution.py:217
  4.3 3.8 %collective-permute-start = (f32[408,128]{1,0:T(8,128)S(1)}, f32[408,128]{1,0:T(8,128)S(1)}, u32[]{:S(2)}, u32[]{:S(2)}) collective-permute-start(f32[408,128]{1,0:T(8,128)S(1)} %get-tuple-element.33), channel_id=1, source_target_pairs={{0,4},{4,8},{8,12},{12,16},{16,20},{20,24},{24,28},{28,32},{32,36}... | collective-permute-start | bytes 626696 | tf_op jit(solution)/shard_map/ppermute | solution.py:262
  8.1 3.6 %shard_map.155 = (f32[400,128]{1,0:T(8,128)S(1)}, f32[1,128]{1,0:T(1,128)S(1)}, f32[2,400,256]{2,1,0:T(8,128)S(1)}, f32[400,512]{1,0:T(8,128)S(1)}, f32[400,256]{1,0:T(8,128)S(1)}, /*index=5*/f32[400,512]{1,0:T(8,128)S(1)}) custom-call(f32[400,128]{1,0:T(8,128)S(1)} %get-tuple-element.34.source, f32[400,128]{1,0:T(8,128)S(1)} %get-tuple-element.35.target, ...), custom_call_target="tpu_custom_call" | custom-call | flops 4000000000 | bytes 4316168 | tf_op jit(solution)/shard_map/pallas_call | solution.py:217
  11.8 0.0 copy-start
  11.8 0.0 collective-permute-done.moved
  11.8 1.8 %shard_map.157 = (f32[800,128]{1,0:T(8,128)S(1)}, f32[800,128]{1,0:T(8,128)S(1)}) custom-call(f32[408,128]{1,0:T(8,128)S(1)} %collective-permute-done.moved, f32[400,512]{1,0:T(8,128)S(1)} %get-tuple-element.45.right, f32[400,256]{1,0:T(8,128)S(1)} %get-tuple-element.46.sampled, f32[400,512]{1,0:T(8,128)S(1)} %get-tuple-element.47.scale, ...), custom_call_target="tpu_custom_call" | custom-call | flops 2000000000 | bytes 3903496 | tf_op jit(solution)/shard_map/pallas_call | solution.py:217
  13.6 0.0 copy-done
  13.6 2.4 %all-gather = f32[1600,128]{1,0:T(8,128)S(1)} all-gather(f32[800,128]{1,0:T(8,128)S(1)} %get-tuple-element.50), channel_id=2, replica_groups=mesh['x'=4,'h'=2,'y'=8,'c'=2,'l'=4] {'c'}, dimensions={0}, use_global_device_ids=true | all-gather | bytes 1228800 | tf_op jit(solution)/shard_map/all_gather | solution.py:270
  16.0 0.8 shard_map.158
  16.8 12.9 %all-to-all-start = ((f32[32,1,3200]{2,1,0:T(1,128)}), f32[32,1,3200]{2,1,0:T(1,128)S(1)}, u32[]{:S(2)}, u32[]{:S(2)}) async-start(f32[32,1,3200]{2,1,0:T(1,128)} %bitcast.10), calls=%async_computation | async-start | bytes 819200 | tf_op jit(solution)/shard_map/all_to_all | solution.py:233
  29.7 0.0 copy-start.1
  29.7 0.9 %copy-done.1 = f32[400,128]{1,0:T(8,128)S(1)} copy-done((f32[400,128]{1,0:T(8,128)S(1)}, f32[400,128]{1,0:T(8,128)}, u32[]{:S(2)}) %copy-start.1) | copy-done | bytes 204824
  30.6 3.2 %shard_map.156 = (f32[400,128]{1,0:T(8,128)}, f32[1,128]{1,0:T(1,128)}, f32[400,128]{1,0:T(8,128)}, f32[1,128]{1,0:T(1,128)}) custom-call(f32[408,128]{1,0:T(8,128)S(1)} %collective-permute-done.moved, f32[400,128]{1,0:T(8,128)S(1)} %copy-done.1, f32[1,128]{1,0:T(1,128)S(1)} %get-tuple-element.44.target_acc, f32[400,512]{1,0:T(8,128)S(1)} %get-tuple-element.45.right, ...), custom_call_target="tpu_custom_call" | custom-call | flops 4000000000 | bytes 2883080 | tf_op jit(solution)/shard_map/pallas_call | solution.py:217
  33.8 6.3 %all-to-all-done = f32[32,1,3200]{2,1,0:T(1,128)S(1)} async-done(((f32[32,1,3200]{2,1,0:T(1,128)}), f32[32,1,3200]{2,1,0:T(1,128)S(1)}, u32[]{:S(2)}, u32[]{:S(2)}) %all-to-all-start) | async-done | bytes 409632 | tf_op jit(solution)/shard_map/all_to_all | solution.py:233
  40.2 17.2 %all_to_all.15 = f32[8,1,3200]{2,1,0:T(1,128)S(1)} all-to-all(f32[8,1,3200]{2,1,0:T(1,128)S(1)} %bitcast.27), channel_id=1, replica_groups={{0,1,2,3,64,65,66,67},{8,9,10,11,72,73,74,75},{16,17,18,19,80,81,82,83}..., dimensions={0} | all-to-all | bytes 204800 | tf_op jit(solution)/shard_map/all_to_all | solution.py:233
  57.4 15.9 %all_to_all.16 = f32[32,1,3200]{2,1,0:T(1,128)S(1)} all-to-all(f32[32,1,3200]{2,1,0:T(1,128)S(1)} %bitcast.26), channel_id=1, replica_groups={{0,8,16,24,32,40,48,56,128,136,144,152,160,168,176,184,256,264,272,280,..., dimensions={0} | all-to-all | bytes 819200 | tf_op jit(solution)/shard_map/all_to_all | solution.py:233
  73.3 7.3 %all_gather.11.sums = f32[1600,128]{1,0:T(8,128)S(1)} all-gather(f32[800,128]{1,0:T(8,128)S(1)} %bitcast.29), channel_id=1, replica_groups=mesh['x'=4,'h'=2,'y'=8,'c'=2,'l'=4] {'c'}, dimensions={0}, use_global_device_ids=true | all-gather | bytes 1228800 | tf_op jit(solution)/shard_map/all_gather | solution.py:285
  80.6 1.2 %shard_map.161 = (f32[400,512]{1,0:T(8,128)}, f32[1,512]{1,0:T(1,128)}) custom-call(f32[1600,128]{1,0:T(8,128)S(1)} %all_gather.11.sums, f32[400,512]{1,0:T(8,128)S(1)} %get-tuple-element.37.relation, f32[1,512]{1,0:T(1,128)S(1)} %get-tuple-element.57.relation_acc), custom_call_target="tpu_custom_call" | custom-call | bytes 2461696 | tf_op jit(solution)/shard_map/pallas_call | solution.py:217
  (2 shorter events, 0.1 us)
Async XLA Ops:
  4.3 7.4 %collective-permute-start = (f32[408,128]{1,0:T(8,128)S(1)}, f32[408,128]{1,0:T(8,128)S(1)}, u32[]{:S(2)}, u32[]{:S(2)}) collective-permute-start(f32[408,128]{1,0:T(8,128)S(1)} %get-tuple-element.33), channel_id=1, source_target_pairs={{0,4},{4,8},{8,12},{12,16},{16,20},{20,24},{24,28},{28,32},{32,36}... | collective-permute-start | bytes 626696 | tf_op jit(solution)/shard_map/ppermute | solution.py:262
  11.8 1.8 %copy-start = (f32[400,128]{1,0:T(8,128)}, f32[400,128]{1,0:T(8,128)S(1)}, u32[]{:S(2)}) copy-start(f32[400,128]{1,0:T(8,128)S(1)} %get-tuple-element.43.target) | copy-start | bytes 614404
  16.8 23.3 %all-to-all-start = ((f32[32,1,3200]{2,1,0:T(1,128)}), f32[32,1,3200]{2,1,0:T(1,128)S(1)}, u32[]{:S(2)}, u32[]{:S(2)}) async-start(f32[32,1,3200]{2,1,0:T(1,128)} %bitcast.10), calls=%async_computation | async-start | bytes 819200 | tf_op jit(solution)/shard_map/all_to_all | solution.py:233
  29.7 0.9 %copy-start.1 = (f32[400,128]{1,0:T(8,128)S(1)}, f32[400,128]{1,0:T(8,128)}, u32[]{:S(2)}) copy-start(f32[400,128]{1,0:T(8,128)} %copy-done) | copy-start | bytes 614404

commit v5 on v4

--- a/solution.py
+++ b/solution.py
@@ -269,17 +269,18 @@
     )
     both = lax.all_gather(sent, "c")
     parts = call(add_received, [blocks], both, kept, pinned=True)[0]
-    source, source_acc, target, target_acc = call(
-        second_rest, [table, row, table, row],
-        moved, target, target_acc, right, sampled, scale, sid, tid, nid, cnt, flops=4 * work,
-    )
     planes, lines = plane_groups(), line_groups()
     in_plane, in_line = len(planes[0]), len(lines[0])
     share = blocks[0] // in_plane
     parts = exchange(parts.reshape(in_plane, 1, -1), planes).reshape(blocks)
     (block,) = call(functools.partial(fold, copies=in_line), [(share * in_line, LANES)], in_vmem(parts))
-    block, source_acc = lax.optimization_barrier((block, source_acc))
+    block, target_acc = lax.optimization_barrier((block, target_acc))
     parts = exchange(block.reshape(in_line, 1, -1), lines).reshape(share * in_line, LANES)
+    source, source_acc, target, target_acc = call(
+        second_rest, [table, row, table, row],
+        moved, target, target_acc, right, sampled, scale, sid, tid, nid, cnt, flops=4 * work,
+    )
+    parts, source_acc = lax.optimization_barrier((parts, source_acc))
     (block,) = call(functools.partial(fold, copies=in_plane), [blocks], in_vmem(parts))
     halves = exchange(block.reshape(in_plane, 1, -1), planes).reshape(blocks)
     sums = lax.all_gather(halves, "c", tiled=True)

time: 82.1 us -> 82.1 us (level)
  blocking collectives: 42.8 us -> 48.1 us
  waiting for transfers between devices: 6.35 us -> 3.21 us
  starting transfers between devices: 16.6 us -> 15.3 us
  local copies, waits for them, and re-layouts: 0.93 us -> 0 us
    all_to_all x2, blocking collectives: 33 us -> 38.8 us  [exchange(): lax.all_to_all(blocks, AXES, 0, 0, axis_index_groups=groups, tiled=True)]
    all_to_all x1, waiting for transfers between devices: 6.35 us -> 3.21 us  [exchange(): lax.all_to_all(blocks, AXES, 0, 0, axis_index_groups=groups, tiled=True)]
    all_to_all x1, starting transfers between devices: 12.9 us -> 11.6 us  [exchange(): lax.all_to_all(blocks, AXES, 0, 0, axis_index_groups=groups, tiled=True)]
    unnamed x4 -> x0, local copies, waits for them, and re-layouts: 0.93 us -> none
where the time goes in v5:
time: 82.1 us; the launch traced here: 81.7 us
  blocking collectives  48.1 us (59%)
  starting transfers between devices  15.3 us (19%)
  Pallas kernels  14.4 us (18%)
  waiting for transfers between devices  3.21 us (4%)
    all_to_all x2, blocking collectives, exchange(): lax.all_to_all(blocks, AXES, 0, 0, axis_index_groups=groups, tiled=True)  38.8 us
    pallas_call x8, Pallas kernels, call(): pl.pallas_call(kernel, out_shape=outs, in_specs=[spec] * len(operands), o...  14.4 us
    all_to_all x1, starting transfers between devices, exchange(): lax.all_to_all(blocks, AXES, 0, 0, axis_index_groups=groups, tiled=True)  11.6 us
    all_gather x1, blocking collectives, on_device(): sums = lax.all_gather(halves, 'c', tiled=True)  6.85 us
    ppermute x1, starting transfers between devices, on_device(): lax.ppermute(moved, BLK, [(i, (i + 1) % count) for i in range(count)])  3.76 us
    all_to_all x1, waiting for transfers between devices, exchange(): lax.all_to_all(blocks, AXES, 0, 0, axis_index_groups=groups, tiled=True)  3.21 us
    all_gather x1, blocking collectives, on_device(): both = lax.all_gather(sent, 'c')  2.39 us
  transfers between devices with their start and end apart: 2, of which 1 were waited for; matrix products, arithmetic and copies ran while one was open for 0% of the time, Pallas kernels for 8%

profile of v5, /device:TPU:9, one launch (start us, length us, event | category | flops | bytes accessed | tf_op | source)
XLA Modules:
  0.0 81.7 jit_solution(4484001105293928789)
XLA Ops:
  0.6 3.7 %shard_map.154 = (f32[408,128]{1,0:T(8,128)S(1)}, s32[2,1,1,512]{3,2,1,0:T(1,128)S(1)}, f32[400,128]{1,0:T(8,128)S(1)}, s32[2,1,1,512]{3,2,1,0:T(1,128)S(1)}, f3...) custom-call(s32[2,1,1,512]{3,2,1,0:T(1,128)} %refs_0_.1, ...), custom_call_target="tpu_custom_call" | custom-call | flops 2000000000 | bytes 2701328 | tf_op jit(solution)/shard_map/pallas_call | solution.py:217
  4.3 3.8 %collective-permute-start = (f32[408,128]{1,0:T(8,128)S(1)}, f32[408,128]{1,0:T(8,128)S(1)}, u32[]{:S(2)}, u32[]{:S(2)}) collective-permute-start(f32[408,128]{1,0:T(8,128)S(1)} %get-tuple-element.35), channel_id=1, source_target_pairs={{0,4},{4,8},{8,12},{12,16},{16,20},{20,24},{24,28},{28,32},{32,36}... | collective-permute-start | bytes 626696 | tf_op jit(solution)/shard_map/ppermute | solution.py:262
  8.1 3.6 %shard_map.155 = (f32[400,128]{1,0:T(8,128)S(1)}, f32[1,128]{1,0:T(1,128)S(1)}, f32[2,400,256]{2,1,0:T(8,128)S(1)}, f32[400,512]{1,0:T(8,128)S(1)}, f32[400,256]{1,0:T(8,128)S(1)}, /*index=5*/f32[400,512]{1,0:T(8,128)S(1)}) custom-call(f32[400,128]{1,0:T(8,128)S(1)} %get-tuple-element.36.source, f32[400,128]{1,0:T(8,128)S(1)} %get-tuple-element.37.target, ...), custom_call_target="tpu_custom_call" | custom-call | flops 4000000000 | bytes 4316168 | tf_op jit(solution)/shard_map/pallas_call | solution.py:217
  11.8 0.0 collective-permute-done.moved
  11.8 1.9 %shard_map.156 = (f32[800,128]{1,0:T(8,128)S(1)}, f32[800,128]{1,0:T(8,128)S(1)}) custom-call(f32[408,128]{1,0:T(8,128)S(1)} %collective-permute-done.moved, f32[400,512]{1,0:T(8,128)S(1)} %get-tuple-element.46.right, f32[400,256]{1,0:T(8,128)S(1)} %get-tuple-element.47.sampled, f32[400,512]{1,0:T(8,128)S(1)} %get-tuple-element.48.scale, ...), custom_call_target="tpu_custom_call" | custom-call | flops 2000000000 | bytes 3903496 | tf_op jit(solution)/shard_map/pallas_call | solution.py:217
  13.6 2.4 %all-gather = f32[1600,128]{1,0:T(8,128)S(1)} all-gather(f32[800,128]{1,0:T(8,128)S(1)} %get-tuple-element.50), channel_id=2, replica_groups=mesh['x'=4,'h'=2,'y'=8,'c'=2,'l'=4] {'c'}, dimensions={0}, use_global_device_ids=true | all-gather | bytes 1228800 | tf_op jit(solution)/shard_map/all_gather | solution.py:270
  16.0 0.1 shard_map.157
  16.1 23.1 %all_to_all.15 = f32[32,1,3200]{2,1,0:T(1,128)S(1)} all-to-all(f32[32,1,3200]{2,1,0:T(1,128)S(1)} %bitcast.25), channel_id=1, replica_groups={{0,8,16,24,32,40,48,56,128,136,144,152,160,168,176,184,256,264,272,280,..., dimensions={0} | all-to-all | bytes 819200 | tf_op jit(solution)/shard_map/all_to_all | solution.py:233
  39.2 0.7 shard_map.158
  39.9 11.6 %all-to-all-start.1 = ((f32[8,1,3200]{2,1,0:T(1,128)}), f32[8,1,3200]{2,1,0:T(1,128)S(1)}, u32[]{:S(2)}, u32[]{:S(2)}) async-start(f32[8,1,3200]{2,1,0:T(1,128)} %bitcast.12), calls=%async_computation.1 | async-start | bytes 204800 | tf_op jit(solution)/shard_map/all_to_all | solution.py:233
  51.5 3.3 %shard_map.159 = (f32[400,128]{1,0:T(8,128)}, f32[1,128]{1,0:T(1,128)}, f32[400,128]{1,0:T(8,128)}, f32[1,128]{1,0:T(1,128)}) custom-call(f32[408,128]{1,0:T(8,128)S(1)} %collective-permute-done.moved, f32[400,128]{1,0:T(8,128)S(1)} %get-tuple-element.45.target, f32[1,128]{1,0:T(1,128)S(1)} %get-tuple-element.53.target_acc, ...), custom_call_target="tpu_custom_call" | custom-call | flops 4000000000 | bytes 2883080 | tf_op jit(solution)/shard_map/pallas_call | solution.py:217
  54.8 3.2 %all-to-all-done.1 = f32[8,1,3200]{2,1,0:T(1,128)S(1)} async-done(((f32[8,1,3200]{2,1,0:T(1,128)}), f32[8,1,3200]{2,1,0:T(1,128)S(1)}, u32[]{:S(2)}, u32[]{:S(2)}) %all-to-all-start.1) | async-done | bytes 102432 | tf_op jit(solution)/shard_map/all_to_all | solution.py:233
  58.0 15.7 %all_to_all.16 = f32[32,1,3200]{2,1,0:T(1,128)S(1)} all-to-all(f32[32,1,3200]{2,1,0:T(1,128)S(1)} %bitcast.27), channel_id=1, replica_groups={{0,8,16,24,32,40,48,56,128,136,144,152,160,168,176,184,256,264,272,280,..., dimensions={0} | all-to-all | bytes 819200 | tf_op jit(solution)/shard_map/all_to_all | solution.py:233
  73.7 6.9 %all_gather.11.sums = f32[1600,128]{1,0:T(8,128)S(1)} all-gather(f32[800,128]{1,0:T(8,128)S(1)} %bitcast.29), channel_id=1, replica_groups=mesh['x'=4,'h'=2,'y'=8,'c'=2,'l'=4] {'c'}, dimensions={0}, use_global_device_ids=true | all-gather | bytes 1228800 | tf_op jit(solution)/shard_map/all_gather | solution.py:286
  80.5 1.2 %shard_map.161 = (f32[400,512]{1,0:T(8,128)}, f32[1,512]{1,0:T(1,128)}) custom-call(f32[1600,128]{1,0:T(8,128)S(1)} %all_gather.11.sums, f32[400,512]{1,0:T(8,128)S(1)} %get-tuple-element.39.relation, f32[1,512]{1,0:T(1,128)S(1)} %get-tuple-element.61.relation_acc), custom_call_target="tpu_custom_call" | custom-call | bytes 2461696 | tf_op jit(solution)/shard_map/pallas_call | solution.py:217
  (1 shorter events, 0.0 us)
Async XLA Ops:
  4.3 7.4 %collective-permute-start = (f32[408,128]{1,0:T(8,128)S(1)}, f32[408,128]{1,0:T(8,128)S(1)}, u32[]{:S(2)}, u32[]{:S(2)}) collective-permute-start(f32[408,128]{1,0:T(8,128)S(1)} %get-tuple-element.35), channel_id=1, source_target_pairs={{0,4},{4,8},{8,12},{12,16},{16,20},{20,24},{24,28},{28,32},{32,36}... | collective-permute-start | bytes 626696 | tf_op jit(solution)/shard_map/ppermute | solution.py:262
  39.9 18.1 %all-to-all-start.1 = ((f32[8,1,3200]{2,1,0:T(1,128)}), f32[8,1,3200]{2,1,0:T(1,128)S(1)}, u32[]{:S(2)}, u32[]{:S(2)}) async-start(f32[8,1,3200]{2,1,0:T(1,128)} %bitcast.12), calls=%async_computation.1 | async-start | bytes 204800 | tf_op jit(solution)/shard_map/all_to_all | solution.py:233

commit v6 on v5

--- a/solution.py
+++ b/solution.py
@@ -75,11 +75,11 @@
     return weights - rate * grads * lax.rsqrt(fresh), fresh
 
 
-def scores(query, right, sampled, count):
-    slots, negatives = query.shape[1], sampled.shape[1]
+def scores(query, right, turned, count):
+    slots, negatives = query.shape[1], turned.shape[0]
     alive = (lax.broadcasted_iota(jnp.int32, (1, slots), 1) < count).astype(F32)
     positive = jnp.sum(query * right, axis=0, keepdims=True)
-    negative = product3(split(sampled.T), split(query))
+    negative = product3(split(turned), split(query))
     pull = -alive * jax.nn.sigmoid(-positive)
     push = jax.nn.sigmoid(negative) * (alive / negatives)
     return pull, push
@@ -90,9 +90,9 @@
     return scatter(pull * query, target_hot) + scatter(to_samples, sample_hot)
 
 
-def bucket(left, right, sampled, scale, cnt):
+def bucket(left, right, sampled, scale, cnt, turned=None):
     query = left * scale
-    pull, push = scores(query, right, sampled, cnt)
+    pull, push = scores(query, right, sampled.T if turned is None else turned, cnt)
     grad_query = pull * right + product3(split(sampled), split(push))
     return query, pull, push, grad_query
 
@@ -122,7 +122,7 @@
 
 def first_rest(
     source, target, target_acc, relation, sid, tid, kid, nid, cnt,
-    target_out, target_acc_out, total, right_out, sampled_out, scale_out,
+    target_out, target_acc_out, total, right_out, sampled_out, scale_out, turned_out,
 ):
     kind_hot = one_hot(kid[0, 0], relation.shape[1])
     target_hot, sample_hot = one_hot(tid[0, 0], LANES), one_hot(nid[0, 0, 0], LANES)
@@ -140,7 +140,9 @@
     total[0] = sums[:, :half]
     total[1] = sums[:, half:]
     right_out[...] = gather(rows, one_hot(tid[1, 0], LANES))
-    sampled_out[...] = gather(rows, one_hot(nid[1, 0, 0], LANES))
+    sampled = gather(rows, one_hot(nid[1, 0, 0], LANES))
+    sampled_out[...] = sampled
+    turned_out[...] = sampled.T
     scale_out[...] = gather(relation[...], one_hot(kid[1, 0], relation.shape[1]))
 
 
@@ -150,10 +152,10 @@
         out[block * width : (block + 1) * width, :] = sums[:, block * LANES : (block + 1) * LANES]
 
 
-def second_edges(moved, right, sampled, scale, sid, kid, cnt, total, sent, kept):
+def second_edges(moved, right, sampled, turned, scale, sid, kid, cnt, total, sent, kept):
     width = right.shape[0]
     left = gather(moved[0:width, :], one_hot(sid[1, 0], LANES))
-    grad_query = bucket(left, right[...], sampled[...], scale[...], cnt[0, :, 1:2])[-1]
+    grad_query = bucket(left, right[...], sampled[...], scale[...], cnt[0, :, 1:2], turned[...])[-1]
     typed = jnp.concatenate(split(grad_query * left), 0)
     me = lax.axis_index("c")
     half = total.shape[2]
@@ -163,13 +165,13 @@
 
 
 def second_rest(
-    moved, target, target_acc, right, sampled, scale, sid, tid, nid, cnt,
+    moved, target, target_acc, right, sampled, turned, scale, sid, tid, nid, cnt,
     source_out, source_acc_out, target_out, target_acc_out,
 ):
     width = target.shape[0]
     source_hot = one_hot(sid[1, 0], LANES)
     left = gather(moved[0:width, :], source_hot)
-    query, pull, push, grad_query = bucket(left, right[...], sampled[...], scale[...], cnt[0, :, 1:2])
+    query, pull, push, grad_query = bucket(left, right[...], sampled[...], scale[...], cnt[0, :, 1:2], turned[...])
     grads = target_grads(query, pull, push, one_hot(tid[1, 0], LANES), one_hot(nid[1, 0, 0], LANES))
     target_out[...], target_acc_out[...] = adagrad(target[...], target_acc[...], grads, learning_rate)
     grads = scatter(grad_query * scale[...], source_hot)
@@ -260,12 +262,12 @@
     )
     count = lax.axis_size(BLK)
     moved = lax.ppermute(moved, BLK, [(i, (i + 1) % count) for i in range(count)])
-    target, target_acc, total, right, sampled, scale = call(
-        first_rest, [table, row, (2, width, kinds // 2), edges, (width, negatives), edges],
+    target, target_acc, total, right, sampled, scale, turned = call(
+        first_rest, [table, row, (2, width, kinds // 2), edges, (width, negatives), edges, (negatives, width)],
         source, target, target_state, relation, sid, tid, kid, nid, cnt, flops=4 * work,
     )
     sent, kept = call(
-        second_edges, [blocks, blocks], moved, right, sampled, scale, sid, kid, cnt, total, flops=2 * work
+        second_edges, [blocks, blocks], moved, right, sampled, turned, scale, sid, kid, cnt, total, flops=2 * work
     )
     both = lax.all_gather(sent, "c")
     parts = call(add_received, [blocks], both, kept, pinned=True)[0]
@@ -278,7 +280,7 @@
     parts = exchange(block.reshape(in_line, 1, -1), lines).reshape(share * in_line, LANES)
     source, source_acc, target, target_acc = call(
         second_rest, [table, row, table, row],
-        moved, target, target_acc, right, sampled, scale, sid, tid, nid, cnt, flops=4 * work,
+        moved, target, target_acc, right, sampled, turned, scale, sid, tid, nid, cnt, flops=4 * work,
     )
     parts, source_acc = lax.optimization_barrier((parts, source_acc))
     (block,) = call(functools.partial(fold, copies=in_plane), [blocks], in_vmem(parts))

time: 82.1 us -> 82.1 us (level)
  local copies, waits for them, and re-layouts: 0 us -> 1.01 us
  waiting for transfers between devices: 3.21 us -> 2.25 us
    unnamed x0 -> x4, local copies, waits for them, and re-layouts: none -> 1.01 us
    all_to_all x1, waiting for transfers between devices: 3.21 us -> 2.24 us  [exchange(): lax.all_to_all(blocks, AXES, 0, 0, axis_index_groups=groups, tiled=True)]
where the time goes in v6:
time: 82.1 us; the launch traced here: 81.7 us
  blocking collectives  48.1 us (59%)
  starting transfers between devices  15.2 us (19%)
  Pallas kernels  14.4 us (18%)
  waiting for transfers between devices  2.25 us (3%)
  local copies, waits for them, and re-layouts  1.01 us (1%)
    all_to_all x2, blocking collectives, exchange(): lax.all_to_all(blocks, AXES, 0, 0, axis_index_groups=groups, tiled=True)  38.9 us
    pallas_call x8, Pallas kernels, call(): pl.pallas_call(kernel, out_shape=outs, in_specs=[spec] * len(operands), o...  14.4 us
    all_to_all x1, starting transfers between devices, exchange(): lax.all_to_all(blocks, AXES, 0, 0, axis_index_groups=groups, tiled=True)  11.4 us
    all_gather x1, blocking collectives, on_device(): sums = lax.all_gather(halves, 'c', tiled=True)  6.85 us
    ppermute x1, starting transfers between devices, on_device(): lax.ppermute(moved, BLK, [(i, (i + 1) % count) for i in range(count)])  3.77 us
    all_gather x1, blocking collectives, on_device(): both = lax.all_gather(sent, 'c')  2.39 us
    all_to_all x1, waiting for transfers between devices, exchange(): lax.all_to_all(blocks, AXES, 0, 0, axis_index_groups=groups, tiled=True)  2.24 us
  transfers between devices with their start and end apart: 2, of which 1 were waited for; matrix products, arithmetic and copies ran while one was open for 0% of the time, Pallas kernels for 8%

profile of v6, /device:TPU:9, one launch (start us, length us, event | category | flops | bytes accessed | tf_op | source)
XLA Modules:
  0.0 81.7 jit_solution(7091703285901815527)
XLA Ops:
  0.6 3.7 %shard_map.154 = (f32[408,128]{1,0:T(8,128)S(1)}, s32[2,1,1,512]{3,2,1,0:T(1,128)S(1)}, f32[400,128]{1,0:T(8,128)S(1)}, s32[2,1,1,512]{3,2,1,0:T(1,128)S(1)}, f3...) custom-call(s32[2,1,1,512]{3,2,1,0:T(1,128)} %refs_0_.1, ...), custom_call_target="tpu_custom_call" | custom-call | flops 2000000000 | bytes 2701328 | tf_op jit(solution)/shard_map/pallas_call | solution.py:219
  4.3 3.8 %collective-permute-start = (f32[408,128]{1,0:T(8,128)S(1)}, f32[408,128]{1,0:T(8,128)S(1)}, u32[]{:S(2)}, u32[]{:S(2)}) collective-permute-start(f32[408,128]{1,0:T(8,128)S(1)} %get-tuple-element.36), channel_id=1, source_target_pairs={{0,4},{4,8},{8,12},{12,16},{16,20},{20,24},{24,28},{28,32},{32,36}... | collective-permute-start | bytes 626696 | tf_op jit(solution)/shard_map/ppermute | solution.py:264
  8.1 3.7 %shard_map.155 = (f32[400,128]{1,0:T(8,128)S(1)}, f32[1,128]{1,0:T(1,128)S(1)}, f32[2,400,256]{2,1,0:T(8,128)S(1)}, f32[400,512]{1,0:T(8,128)S(1)}, f32[400,256]...) custom-call(f32[400,128]{1,0:T(8,128)S(1)} %get-tuple-element.37.source, ...), custom_call_target="tpu_custom_call" | custom-call | flops 4000000000 | bytes 4725768 | tf_op jit(solution)/shard_map/pallas_call | solution.py:219
  11.8 0.0 copy-start
  11.8 0.0 collective-permute-done.moved
  11.8 1.8 %shard_map.156 = (f32[800,128]{1,0:T(8,128)S(1)}, f32[800,128]{1,0:T(8,128)S(1)}) custom-call(f32[408,128]{1,0:T(8,128)S(1)} %collective-permute-done.moved, f32[400,512]{1,0:T(8,128)S(1)} %get-tuple-element.47.right, f32[400,256]{1,0:T(8,128)S(1)} %get-tuple-element.48.sampled, f32[256,400]{1,0:T(8,128)S(1)} %get-tuple-element.49.turned, ...), custom_call_target="tpu_custom_call" | custom-call | flops 2000000000 | bytes 4313096 | tf_op jit(solution)/shard_map/pallas_call | solution.py:219
  13.7 0.0 copy-done
  13.7 2.4 %all-gather = f32[1600,128]{1,0:T(8,128)S(1)} all-gather(f32[800,128]{1,0:T(8,128)S(1)} %get-tuple-element.52), channel_id=2, replica_groups=mesh['x'=4,'h'=2,'y'=8,'c'=2,'l'=4] {'c'}, dimensions={0}, use_global_device_ids=true | all-gather | bytes 1228800 | tf_op jit(solution)/shard_map/all_gather | solution.py:272
  16.1 0.1 shard_map.157
  16.1 23.2 %all_to_all.15 = f32[32,1,3200]{2,1,0:T(1,128)S(1)} all-to-all(f32[32,1,3200]{2,1,0:T(1,128)S(1)} %bitcast.25), channel_id=1, replica_groups={{0,8,16,24,32,40,48,56,128,136,144,152,160,168,176,184,256,264,272,280,..., dimensions={0} | all-to-all | bytes 819200 | tf_op jit(solution)/shard_map/all_to_all | solution.py:235
  39.3 0.7 shard_map.158
  40.0 11.4 %all-to-all-start.1 = ((f32[8,1,3200]{2,1,0:T(1,128)}), f32[8,1,3200]{2,1,0:T(1,128)S(1)}, u32[]{:S(2)}, u32[]{:S(2)}) async-start(f32[8,1,3200]{2,1,0:T(1,128)} %bitcast.12), calls=%async_computation.1 | async-start | bytes 204800 | tf_op jit(solution)/shard_map/all_to_all | solution.py:235
  51.5 0.0 copy-start.1
  51.5 1.0 %copy-done.1 = f32[400,256]{1,0:T(8,128)S(1)} copy-done((f32[400,256]{1,0:T(8,128)S(1)}, f32[400,256]{1,0:T(8,128)}, u32[]{:S(2)}) %copy-start.1) | copy-done | bytes 409624
  52.5 3.2 %shard_map.159 = (f32[400,128]{1,0:T(8,128)}, f32[1,128]{1,0:T(1,128)}, f32[400,128]{1,0:T(8,128)}, f32[1,128]{1,0:T(1,128)}) custom-call(f32[408,128]{1,0:T(8,128)S(1)} %collective-permute-done.moved, f32[400,128]{1,0:T(8,128)S(1)} %get-tuple-element.46.target, f32[1,128]{1,0:T(1,128)S(1)} %get-tuple-element.55.target_acc, ...), custom_call_target="tpu_custom_call" | custom-call | flops 4000000000 | bytes 3292680 | tf_op jit(solution)/shard_map/pallas_call | solution.py:219
  55.7 2.2 %all-to-all-done.1 = f32[8,1,3200]{2,1,0:T(1,128)S(1)} async-done(((f32[8,1,3200]{2,1,0:T(1,128)}), f32[8,1,3200]{2,1,0:T(1,128)S(1)}, u32[]{:S(2)}, u32[]{:S(2)}) %all-to-all-start.1) | async-done | bytes 102432 | tf_op jit(solution)/shard_map/all_to_all | solution.py:235
  58.0 15.7 %all_to_all.16 = f32[32,1,3200]{2,1,0:T(1,128)S(1)} all-to-all(f32[32,1,3200]{2,1,0:T(1,128)S(1)} %bitcast.27), channel_id=1, replica_groups={{0,8,16,24,32,40,48,56,128,136,144,152,160,168,176,184,256,264,272,280,..., dimensions={0} | all-to-all | bytes 819200 | tf_op jit(solution)/shard_map/all_to_all | solution.py:235
  73.7 6.9 %all_gather.11.sums = f32[1600,128]{1,0:T(8,128)S(1)} all-gather(f32[800,128]{1,0:T(8,128)S(1)} %bitcast.29), channel_id=1, replica_groups=mesh['x'=4,'h'=2,'y'=8,'c'=2,'l'=4] {'c'}, dimensions={0}, use_global_device_ids=true | all-gather | bytes 1228800 | tf_op jit(solution)/shard_map/all_gather | solution.py:288
  80.5 1.2 %shard_map.161 = (f32[400,512]{1,0:T(8,128)}, f32[1,512]{1,0:T(1,128)}) custom-call(f32[1600,128]{1,0:T(8,128)S(1)} %all_gather.11.sums, f32[400,512]{1,0:T(8,128)S(1)} %get-tuple-element.40.relation, f32[1,512]{1,0:T(1,128)S(1)} %get-tuple-element.63.relation_acc), custom_call_target="tpu_custom_call" | custom-call | bytes 2461696 | tf_op jit(solution)/shard_map/pallas_call | solution.py:219
  (1 shorter events, 0.0 us)
Async XLA Ops:
  4.3 7.5 %collective-permute-start = (f32[408,128]{1,0:T(8,128)S(1)}, f32[408,128]{1,0:T(8,128)S(1)}, u32[]{:S(2)}, u32[]{:S(2)}) collective-permute-start(f32[408,128]{1,0:T(8,128)S(1)} %get-tuple-element.36), channel_id=1, source_target_pairs={{0,4},{4,8},{8,12},{12,16},{16,20},{20,24},{24,28},{28,32},{32,36}... | collective-permute-start | bytes 626696 | tf_op jit(solution)/shard_map/ppermute | solution.py:264
  11.8 1.9 %copy-start = (f32[400,256]{1,0:T(8,128)}, f32[400,256]{1,0:T(8,128)S(1)}, u32[]{:S(2)}) copy-start(f32[400,256]{1,0:T(8,128)S(1)} %get-tuple-element.48.sampled) | copy-start | bytes 1228804
  40.0 17.9 %all-to-all-start.1 = ((f32[8,1,3200]{2,1,0:T(1,128)}), f32[8,1,3200]{2,1,0:T(1,128)S(1)}, u32[]{:S(2)}, u32[]{:S(2)}) async-start(f32[8,1,3200]{2,1,0:T(1,128)} %bitcast.12), calls=%async_computation.1 | async-start | bytes 204800 | tf_op jit(solution)/shard_map/all_to_all | solution.py:235
  51.5 1.0 %copy-start.1 = (f32[400,256]{1,0:T(8,128)S(1)}, f32[400,256]{1,0:T(8,128)}, u32[]{:S(2)}) copy-start(f32[400,256]{1,0:T(8,128)} %copy-done) | copy-start | bytes 1228804
